TPU v7x, 32 devices: a whole 2x2x4 slice. The times are simulated.
32 devices in a mesh: grp: 4 (over y, x), seq: 8 (over z, core).
Axes of the slice: x: 2, y: 2, z: 4, core: 2. Of those that a mesh axis runs over, the one named last changes fastest.
Arguments:
- query_input: bfloat16 [4096, 4096], P(('grp', 'seq')), may hold values from -8 to 8
- key_input: bfloat16 [4096, 512], P(('grp', 'seq')), may hold values from -8 to 8
- value_input: bfloat16 [4096, 512], P(('grp', 'seq')), may hold values from -6 to 6
- out_grad: bfloat16 [4096, 4096], P(('grp', 'seq')), may hold values from -6 to 6
- key_blocks: int32 [32, 12], replicated, may hold values from 0 to 31, as said below
- key_counts: int32 [32], replicated, may hold values from 1 to 12, as said below
- block_position: int32 [32], replicated, may hold values from 0 to 31, each once
Outputs:
- attn_out: bfloat16 [4096, 4096], P(('grp', 'seq'))
- query_grad: bfloat16 [4096, 4096], P(('grp', 'seq'))
- key_grad: bfloat16 [4096, 512], P(('grp', 'seq'))
- value_grad: bfloat16 [4096, 512], P(('grp', 'seq'))
Inputs may be any that keep to these rules, and one draw needn't show every extreme that they name: `key_blocks`: in row b the first key_counts[b] entries are distinct, the first is b itself and the others are earlier blocks of the same group of 8 blocks or of the group before; the remaining entries equal b. `key_counts`: the last block's count is 12.
All inputs are finite; a program needn't handle non-finite values.
Results may differ from a plain program's by a relative error of at most 0.015.
Values may be sent and summed in bfloat16 or wider, within the bound.
No kernel may reach another device: no remote copies, remote signals or barrier semaphores. Data moves between devices by JAX's collectives and lax.ppermute only.
A program may use at most 128 MiB of HBM per device.

v0:
```python
import functools
import math

import jax
import jax.numpy as jnp
import numpy as np
from jax import lax
from jax.experimental import pallas as pl
from jax.experimental.pallas import tpu as pltpu
from jax.sharding import PartitionSpec as P

HEADS = 32
KV_HEADS = 4
HEAD_DIM = 128
BLK = 128
CORES = 2
RATIO = HEADS // KV_HEADS
HALF_KV = KV_HEADS // CORES
ROWS = RATIO * BLK
SCALE = 1.0 / math.sqrt(HEAD_DIM)
TO_LOG2 = SCALE * math.log2(math.e)
F32 = jnp.float32
BF16 = jnp.bfloat16
CHUNK = 256

VMEM_SPEC = pl.BlockSpec(memory_space=pltpu.VMEM)
HBM_SPEC = pl.BlockSpec(memory_space=pltpu.HBM)
SMEM_SPEC = pl.BlockSpec(memory_space=pltpu.SMEM)


def trig_table(n_blocks):
    half = HEAD_DIM // 2
    frequency = np.power(500000.0, -np.arange(half) * (2.0 / HEAD_DIM))
    parts = []
    for places in (np.arange(n_blocks) * BLK, np.arange(BLK)):
        angles = places[:, None] * frequency
        for part in (np.cos(angles), np.sin(angles)):
            parts.append(np.concatenate([part, part], axis=1))
    return np.concatenate(parts, axis=0).astype(np.float32)


def block_tables(place, table):
    n_blocks = table.shape[0] // 2 - BLK
    cos_b = table[pl.ds(place, 1), :]
    sin_b = table[pl.ds(n_blocks + place, 1), :]
    cos_t = table[2 * n_blocks : 2 * n_blocks + BLK, :]
    sin_t = table[2 * n_blocks + BLK :, :]
    cosine = cos_b * cos_t - sin_b * sin_t
    sine = sin_b * cos_t + cos_b * sin_t
    lanes = lax.broadcasted_iota(jnp.int32, sine.shape, 1)
    return cosine, jnp.where(lanes < HEAD_DIM // 2, -sine, sine)


def turn(values, cosine, signed_sine):
    return values * cosine + pltpu.roll(values, HEAD_DIM // 2, 1) * signed_sine


def dot_nt(a, b):
    return lax.dot_general(a, b, (((1,), (1,)), ((), ())), preferred_element_type=F32)


def dot_nn(a, b):
    return lax.dot_general(a, b, (((1,), (0,)), ((), ())), preferred_element_type=F32)


def here(n_seq):
    member = lax.axis_index("seq")
    group = lax.axis_index("grp")
    return group, member, lax.rem(member, CORES)


def size_of(array):
    return math.prod(array.shape) * jnp.dtype(array.dtype).itemsize


def call(kernel, out_shape, n_smem, scratch=(), us=1, name=None, spare=6, n_hbm=0, hbm_out=None):
    def run(*arrays):
        n_left = n_smem + n_hbm
        outs = list(out_shape) if isinstance(out_shape, (tuple, list)) else [out_shape]
        held = sum(size_of(a) for a in arrays[n_left:])
        held += sum(size_of(a) for n, a in enumerate(outs) if n != hbm_out)
        held += sum(size_of(a) for a in scratch if a.dtype in (F32, BF16))
        out_specs = [HBM_SPEC if n == hbm_out else VMEM_SPEC for n in range(len(outs))]
        in_specs = [SMEM_SPEC] * n_smem + [HBM_SPEC] * n_hbm
        in_specs += [VMEM_SPEC] * (len(arrays) - n_left)
        pinned = [
            pltpu.with_memory_space_constraint(a, pltpu.HBM) if n < n_left else a
            for n, a in enumerate(arrays)
        ]
        results = pl.pallas_call(
            kernel,
            out_shape=[
                pltpu.HBM(a.shape, a.dtype) if n == hbm_out else a for n, a in enumerate(outs)
            ],
            in_specs=in_specs,
            out_specs=out_specs,
            scratch_shapes=list(scratch),
            compiler_params=pltpu.CompilerParams(vmem_limit_bytes=held + spare * 2**20),
            cost_estimate=pl.CostEstimate(
                flops=us * 10**9, bytes_accessed=2**20, transcendentals=0
            ),
            name=name,
        )(*pinned)
        return results if isinstance(out_shape, (tuple, list)) else results[0]

    return run


def fetch(sources, places, sems):
    copies = [
        pltpu.make_async_copy(source, place, sems.at[n])
        for n, (source, place) in enumerate(zip(sources, places))
    ]
    for copy in copies:
        copy.start()
    for copy in copies:
        copy.wait()


def prepare_kv(n_seq, place_ref, *refs):
    sources, (keep, send), (key, value, table, sems) = refs[:3], refs[3:5], refs[5:]
    fetch(sources, (key, value, table), sems)
    group, member, core = here(n_seq)
    cosine, sine = block_tables(place_ref[group * n_seq + member], table)
    for out, half in ((keep, core), (send, 1 - core)):
        for h in range(HALF_KV):
            columns = pl.ds(pl.multiple_of((half * HALF_KV + h) * HEAD_DIM, HEAD_DIM), HEAD_DIM)
            out[0, h] = turn(key[:, columns].astype(F32), cosine, sine).astype(BF16)
            out[1, h] = value[:, columns]


def prepare_queries(n_seq, place_ref, *refs):
    sources, (keep, send), (query, grad, table, sems) = refs[:3], refs[3:5], refs[5:]
    fetch(sources, (query, grad, table), sems)
    group, member, core = here(n_seq)
    cosine, sine = block_tables(place_ref[group * n_seq + member], table)
    for out, half in ((keep, core), (send, 1 - core)):
        for h in range(HALF_KV):
            for r in range(RATIO):
                head = (half * HALF_KV + h) * RATIO + r
                columns = pl.ds(pl.multiple_of(head * HEAD_DIM, HEAD_DIM), HEAD_DIM)
                out[0, h, r] = turn(query[:, columns].astype(F32), cosine, sine).astype(BF16)
                out[1, h, r] = grad[:, columns]


def list_blocks(
    n_seq, side, block, group, member, key_blocks, key_counts, found, start=0, shift=0
):
    base = (group - 1 + side) * n_seq

    def look(j, n):
        offset = key_blocks[block, j] - base
        hit = jnp.logical_and(offset >= 0, offset < n_seq)

        @pl.when(hit)
        def _():
            found[n] = lax.bitwise_xor(offset, member) + shift

        return n + hit.astype(jnp.int32)

    return lax.fori_loop(1, key_counts[block], look, jnp.int32(start))


def causal():
    keys = lax.broadcasted_iota(jnp.int32, (BLK, CHUNK), 0)
    tokens = lax.rem(lax.broadcasted_iota(jnp.int32, (BLK, CHUNK), 1), BLK)
    return keys <= tokens


def chunks():
    per = CHUNK // BLK
    return [
        (slice(c * per, (c + 1) * per), slice(c * CHUNK, (c + 1) * CHUNK))
        for c in range(ROWS // CHUNK)
    ]


def heads_of(block, what, h, rows):
    return block[what, h, rows].reshape(CHUNK, HEAD_DIM)


def fill(store, pieces, first=0):
    for k, piece in enumerate(pieces):
        store[first + CORES * k : first + CORES * (k + 1)] = piece[...]


def pair_scores(store, e, h, block, rows, diagonal):
    scores = dot_nt(store[e, 0, h], heads_of(block, 0, h, rows))
    if diagonal:
        scores = jnp.where(causal(), scores, -1e30)
    return scores, dot_nt(store[e, 1, h], heads_of(block, 1, h, rows))


def gather_stats(store, e, block, stats, i, diagonal, kept=None):
    for h in range(HALF_KV):
        for rows, columns in chunks():
            scores, dprobs = pair_scores(store, e, h, block, rows, diagonal)
            if kept is not None:
                n, kept_scores, kept_dprobs = kept
                kept_scores[n, h, :, columns] = scores
                kept_dprobs[n, h, :, columns] = dprobs
            top = jnp.max(scores, axis=0, keepdims=True)
            if not diagonal:
                old_top = stats[i, h, 0:1, columns]
                top = jnp.maximum(top, old_top)
            weights = jnp.exp2((scores - top) * TO_LOG2)
            total = jnp.sum(weights, axis=0, keepdims=True)
            mixed = jnp.sum(weights * dprobs, axis=0, keepdims=True)
            if not diagonal:
                shrink = jnp.exp2((old_top - top) * TO_LOG2)
                total += stats[i, h, 1:2, columns] * shrink
                mixed += stats[i, h, 2:3, columns] * shrink
            stats[i, h, 0:1, columns] = top
            stats[i, h, 1:2, columns] = total
            stats[i, h, 2:3, columns] = mixed


def spread_grads(found, count, kept_scores, kept_dprobs, stats, i, block, acc, saved, low, sent):
    def copy(n):
        return pltpu.make_async_copy(low.at[n], saved.at[i, n], sent.at[n])

    def add(n, _):
        e = found[n]
        for h in range(HALF_KV):
            dk, dv = acc[e, 0, h], acc[e, 1, h]
            for rows, columns in chunks():
                probs = jnp.exp2(
                    kept_scores[n, h, :, columns] * TO_LOG2 - stats[i, h, 0:1, columns]
                )
                dscores = probs * (kept_dprobs[n, h, :, columns] - stats[i, h, 2:3, columns])
                probs, dscores = probs.astype(BF16), dscores.astype(BF16)
                low[n, h, 0, :, columns] = probs
                low[n, h, 1, :, columns] = dscores
                dv += dot_nn(probs, heads_of(block, 1, h, rows))
                dk += dot_nn(dscores, heads_of(block, 0, h, rows))
            acc[e, 0, h] = dk
            acc[e, 1, h] = dv
        copy(n).start()
        return 0

    def finish(n, _):
        copy(n).wait()
        return 0

    lax.fori_loop(0, count, add, 0)
    lax.fori_loop(0, count, finish, 0)


def write_grads(acc, outs):
    for k, out in enumerate(outs):
        part = slice(CORES * k, CORES * (k + 1))
        out[:, 0] = (acc[part, 0] * SCALE).astype(out.dtype)
        out[:, 1] = acc[part, 1].astype(out.dtype)


def current_stats(n_seq, key_blocks, key_counts, own, other, *rest):
    n_pieces = n_seq // CORES
    pieces, (stats, store, found) = rest[:n_pieces], rest[n_pieces:]
    group, member, _ = here(n_seq)
    fill(store, pieces)
    for i, block in enumerate((own, other)):
        gather_stats(store, i, block, stats, i, True)
        count = list_blocks(
            n_seq, 1, group * n_seq + lax.bitwise_xor(member, i), group, member,
            key_blocks, key_counts, found,
        )

        def step(n, _):
            gather_stats(store, found[n], block, stats, i, False)
            return 0

        lax.fori_loop(0, count, step, 0)


def previous_grads(n_seq, key_blocks, key_counts, own, other, stats_in, *rest):
    n_pieces = n_seq // CORES
    pieces, outs = rest[:n_pieces], rest[n_pieces : 2 * n_pieces]
    saved, stats, store, found, kept_scores, kept_dprobs, acc, low, sent = rest[2 * n_pieces :]
    group, member, _ = here(n_seq)
    fill(store, pieces)
    acc[...] = jnp.zeros_like(acc)
    stats[...] = stats_in[...]
    for i, block in enumerate((own, other)):
        count = list_blocks(
            n_seq, 0, group * n_seq + lax.bitwise_xor(member, i), group, member,
            key_blocks, key_counts, found,
        )

        def look(n, _):
            gather_stats(store, found[n], block, stats, i, False, (n, kept_scores, kept_dprobs))
            return 0

        lax.fori_loop(0, count, look, 0)
        for h in range(HALF_KV):
            total = stats[i, h, 1:2, :]
            stats[i, h, 0:1, :] = stats[i, h, 0:1, :] * TO_LOG2 + jnp.log2(total)
            stats[i, h, 2:3, :] = stats[i, h, 2:3, :] / total

        spread_grads(
            found, count, kept_scores, kept_dprobs, stats, i, block, acc, saved, low, sent
        )
    write_grads(acc, outs)


def current_grads(n_seq, key_blocks, key_counts, own, other, stats, *rest):
    n_pieces = n_seq // CORES
    pieces, outs = rest[:n_pieces], rest[n_pieces : 2 * n_pieces]
    saved, store, found, kept_scores, kept_dprobs, acc, low, sent = rest[2 * n_pieces :]
    group, member, _ = here(n_seq)
    fill(store, pieces)
    acc[...] = jnp.zeros_like(acc)
    for i, block in enumerate((own, other)):
        found[0] = i
        count = list_blocks(
            n_seq, 1, group * n_seq + lax.bitwise_xor(member, i), group, member,
            key_blocks, key_counts, found, 1,
        )

        def look(n, diagonal):
            for h in range(HALF_KV):
                for rows, columns in chunks():
                    scores, dprobs = pair_scores(store, found[n], h, block, rows, diagonal)
                    kept_scores[n, h, :, columns] = scores
                    kept_dprobs[n, h, :, columns] = dprobs
            return 0

        look(0, True)
        lax.fori_loop(1, count, lambda n, _: look(n, False), 0)
        spread_grads(
            found, count, kept_scores, kept_dprobs, stats, i, block, acc, saved, low, sent
        )
    write_grads(acc, outs)


def query_results(n_seq, h, key_blocks, key_counts, place_ref, far_saved, near_saved, *rest):
    n_pieces = n_seq // CORES
    pieces = rest[: 2 * n_pieces]
    (
        table, own_out, other_out, store, found, low, out_acc, dq_acc, got
    ) = rest[2 * n_pieces :]
    group, member, _ = here(n_seq)
    outs = (own_out, other_out)

    def far_copy(i, n, _):
        return pltpu.make_async_copy(far_saved.at[i, n, h], low.at[i, n], got.at[i, n])

    def near_copy(i, n, count):
        return pltpu.make_async_copy(near_saved.at[i, n - count, h], low.at[i, n], got.at[i, n])

    counts = []
    for i in range(2):
        block = group * n_seq + lax.bitwise_xor(member, i)
        lists = (block, group, member, key_blocks, key_counts, found.at[i])
        far = list_blocks(n_seq, 0, *lists)
        found[i, far] = n_seq + i
        total = list_blocks(n_seq, 1, *lists, far + 1, n_seq)
        counts.append((far, total))

        def fetch_far(n, _):
            far_copy(i, n, 0).start()
            return 0

        def fetch_near(n, _):
            near_copy(i, n, far).start()
            return 0

        lax.fori_loop(0, far, fetch_far, 0)
        lax.fori_loop(far, total, fetch_near, 0)
    for k, piece in enumerate(pieces):
        store[CORES * k : CORES * (k + 1)] = piece[:, :, h : h + 1]
    for i, (far, total) in enumerate(counts):
        mine = group * n_seq + lax.bitwise_xor(member, i)

        @pl.when(lax.rem(total, 2) == 1)
        def _():
            found[i, total] = 0
            low[i, total] = jnp.zeros((2, BLK, ROWS), BF16)

        out_acc[...] = jnp.zeros_like(out_acc)
        dq_acc[...] = jnp.zeros_like(dq_acc)

        def add(n, _):
            pair = (2 * n, 2 * n + 1)
            for m in pair:

                @pl.when(m < far)
                def _():
                    far_copy(i, m, 0).wait()

                @pl.when(jnp.logical_and(m >= far, m < total))
                def _():
                    near_copy(i, m, far).wait()

            keys_t = jnp.concatenate([store[found[i, m], 0, 0].T for m in pair], axis=1)
            values_t = jnp.concatenate([store[found[i, m], 1, 0].T for m in pair], axis=1)
            for _, columns in chunks():
                probs = jnp.concatenate([low[i, m, 0, :, columns] for m in pair], axis=0)
                dscores = jnp.concatenate([low[i, m, 1, :, columns] for m in pair], axis=0)
                out_acc[:, columns] += dot_nn(values_t, probs)
                dq_acc[:, columns] += dot_nn(keys_t, dscores)
            return 0

        lax.fori_loop(0, lax.div(total + 1, 2), add, 0)
        cosine, sine = block_tables(place_ref[mine], table)
        cosine, sine = cosine.T * SCALE, sine.T * SCALE
        for r in range(RATIO):
            rows = slice(r * BLK, (r + 1) * BLK)
            columns = slice(r * HEAD_DIM, (r + 1) * HEAD_DIM)
            outs[i][0, :, columns] = out_acc[:, rows].astype(BF16).T
            dq = dq_acc[:, rows]
            half = HEAD_DIM // 2
            turned = jnp.concatenate([dq[half:], dq[:half]], axis=0)
            outs[i][1, :, columns] = (dq * cosine - turned * sine).astype(BF16).T


def finish_kv(n_seq, place_ref, *rest):
    *terms, table, keep, send = rest
    group, member, _ = here(n_seq)
    for i, result in enumerate((keep, send)):
        offset = lax.bitwise_xor(member, i)
        cosine, sine = block_tables(place_ref[group * n_seq + offset], table)
        for h in range(HALF_KV):
            columns = slice(h * HEAD_DIM, (h + 1) * HEAD_DIM)
            dk, dv = (sum(term[i, w, h].astype(F32) for term in terms) for w in range(2))
            result[0, :, columns] = turn(dk, cosine, -sine).astype(BF16)
            result[1, :, columns] = dv.astype(BF16)


def join_halves(n_parts, *refs):
    parts, outs = refs[: 2 * n_parts], refs[2 * n_parts :]
    core = lax.rem(lax.axis_index("seq"), CORES)
    width = parts[0].shape[-1]
    for half, which in ((core, parts[:n_parts]), (1 - core, parts[n_parts:])):
        for n, part in enumerate(which):
            start = pl.multiple_of((half * n_parts + n) * width, width)
            for w, out in enumerate(outs):
                out[:, pl.ds(start, width)] = part[w]


def local(query_input, key_input, value_input, out_grad, key_blocks, key_counts, block_position):
    n_seq = lax.axis_size("seq")
    n_grp = lax.axis_size("grp")
    n_pieces = n_seq // CORES
    n_listed = key_blocks.shape[1]

    def cross(array, by):
        return lax.ppermute(array, "seq", [(m, m ^ by) for m in range(n_seq)])

    def along(array, by):
        return cross(array, CORES * by)

    def onward(array):
        return lax.ppermute(array, "grp", [(g, g + 1) for g in range(n_grp - 1)])

    def back(array):
        return lax.ppermute(array, "grp", [(g + 1, g) for g in range(n_grp - 1)])

    table = trig_table(block_position.shape[0])
    n_far = min(n_seq, n_listed - 1)
    piece = (2, HALF_KV, BLK, HEAD_DIM)
    chip = (CORES, *piece)
    q_shape = jax.ShapeDtypeStruct((2, HALF_KV, RATIO, BLK, HEAD_DIM), BF16)
    kv_shape = jax.ShapeDtypeStruct(piece, BF16)
    stats_shape = jax.ShapeDtypeStruct((2, HALF_KV, 8, ROWS), F32)
    found = pltpu.SMEM((n_listed,), jnp.int32)
    store = pltpu.VMEM((n_seq, *piece), BF16)
    acc = pltpu.VMEM((n_seq, *piece), F32)
    low = jax.ShapeDtypeStruct(chip, BF16)
    high = jax.ShapeDtypeStruct(chip, F32)

    def prepared(kernel, shape, first, second, name):
        held = [pltpu.VMEM(a.shape, a.dtype) for a in (first, second, table)]
        return call(
            functools.partial(kernel, n_seq), (shape, shape), 1,
            [*held, pltpu.SemaphoreType.DMA((3,))], us=1, name=name, n_hbm=3,
        )(block_position, first, second, table)

    kv_keep, kv_send = prepared(prepare_kv, kv_shape, key_input, value_input, "rotate_keys")
    kv_got = cross(kv_send, 1)
    query_late, kv_keep = lax.optimization_barrier((query_input, kv_keep))
    q_keep, q_send = prepared(prepare_queries, q_shape, query_late, out_grad, "rotate_queries")
    q_send, q_keep, kv_got, kv_keep = lax.optimization_barrier((q_send, q_keep, kv_got, kv_keep))
    q_got = cross(q_send, 1)
    near = [jnp.stack([kv_keep, kv_got])]
    near += [along(near[0], 1)]
    ready, first_far = lax.optimization_barrier((near[1], onward(near[0])))
    far = [first_far, onward(ready)]
    for k in range(2, n_pieces, 2):
        piece_k, _ = lax.optimization_barrier((along(near[0], k), ready))
        near.append(piece_k)
        far.append(onward(near[k]))
        near.append(along(near[k], 1))
        far.append(along(far[k], 1))

    stats = call(
        functools.partial(current_stats, n_seq), stats_shape, 2, [store, found],
        us=6, name="current_statistics",
    )(key_blocks, key_counts, q_keep, q_got, *near)

    def grads_call(kernel, n_slots, outs, us, name):
        kept = pltpu.VMEM((n_slots, HALF_KV, BLK, ROWS), F32)
        pair = (n_slots, HALF_KV, 2, BLK, ROWS)
        saved = jax.ShapeDtypeStruct((2, *pair), BF16)
        return call(
            functools.partial(kernel, n_seq), (*outs[:n_pieces], saved, *outs[n_pieces:]), 2,
            [
                store, found, kept, kept, acc, pltpu.VMEM(pair, BF16),
                pltpu.SemaphoreType.DMA((n_slots,)),
            ],
            us=us, name=name, hbm_out=n_pieces,
        )

    *far_grads, far_saved, stats = grads_call(
        previous_grads, n_far, (low,) * n_pieces + (stats_shape,), 14, "previous_gradients"
    )(key_blocks, key_counts, q_keep, q_got, stats, *far)
    *near_grads, near_saved = grads_call(
        current_grads, min(n_seq, n_listed),
        tuple(low if k % 2 and k > 1 else high for k in range(n_pieces)), 10, "current_gradients",
    )(key_blocks, key_counts, q_keep, q_got, stats, *near)

    half_out = jax.ShapeDtypeStruct((2, BLK, RATIO * HEAD_DIM), BF16)

    def results(h, after):
        place_late, _ = lax.optimization_barrier((block_position, after))
        wide = pltpu.VMEM((HEAD_DIM, ROWS), F32)
        return call(
            functools.partial(query_results, n_seq, h), (half_out, half_out), 3,
            [
                pltpu.VMEM((2 * n_seq, 2, 1, BLK, HEAD_DIM), BF16),
                pltpu.SMEM((2, n_listed + 1), jnp.int32),
                pltpu.VMEM((2, n_listed + 1, 2, BLK, ROWS), BF16), wide, wide,
                pltpu.SemaphoreType.DMA((2, n_listed)),
            ],
            us=20, name="query_results", n_hbm=2,
        )(key_blocks, key_counts, place_late, far_saved, near_saved, *far, *near, table)

    def total(*terms):
        return sum(term.astype(F32) for term in terms).astype(BF16)

    arrived = [back(far_grads[1])]
    last = far_grads[0]
    for k in range(2, n_pieces, 2):
        gathered = total(far_grads[k], along(far_grads[k + 1], 1))
        last, gathered = lax.optimization_barrier((last, gathered))
        arrived.append(back(gathered))
    last = back(last)
    merged = [total(near_grads[1], arrived[0])]
    own_halves, other_halves = [None, None], [None, None]
    own_halves[0], other_halves[0] = results(0, merged[0])
    for n, k in enumerate(range(2, n_pieces, 2)):
        ready, _ = lax.optimization_barrier((near_grads[k], other_halves[0]))
        merged.append(total(ready, arrived[1 + n], along(near_grads[k + 1], 1)))
    own_halves[1], other_halves[1] = results(1, merged[1:])
    got_halves = [cross(half, 1) for half in other_halves]
    final = [near_grads[0], last, along(merged[0], 1)]
    final += [along(merged[1 + n], k) for n, k in enumerate(range(2, n_pieces, 2))]
    final[0], own_halves[1] = lax.optimization_barrier((final[0], own_halves[1]))
    full = jax.ShapeDtypeStruct(query_input.shape, BF16)
    out_rows, query_grad = call(
        functools.partial(join_halves, HALF_KV), (full, full), 0, us=2, name="join_queries"
    )(*own_halves, *got_halves)
    kv_half = jax.ShapeDtypeStruct((2, BLK, HALF_KV * HEAD_DIM), BF16)
    own_kv, other_kv = call(
        functools.partial(finish_kv, n_seq), (kv_half, kv_half), 1,
        us=2, name="key_gradients",
    )(block_position, *final, table)
    got_kv = cross(other_kv, 1)
    full = jax.ShapeDtypeStruct(key_input.shape, BF16)
    key_grad, value_grad = call(
        functools.partial(join_halves, 1), (full, full), 0, us=1, name="join_keys"
    )(own_kv, got_kv)
    return (out_rows, query_grad, key_grad, value_grad)


def solution(mesh):
    split = P(("grp", "seq"), None)
    return jax.shard_map(
        local,
        mesh=mesh,
        in_specs=(split, split, split, split, P(), P(), P()),
        out_specs=(split, split, split, split),
        check_vma=False,
    )
```

profile of v0, /device:TPU:5, one launch (start us, length us, event | category | flops | bytes accessed | tf_op | source)
XLA Modules:
  0.0 104.4 jit_solution(1984536353586702838)
XLA Ops:
  0.6 1.9 %rotate_keys.1 = (bf16[2,2,128,128]{3,2,1,0:T(8,128)(2,1)S(1)}, bf16[2,2,128,128]{3,2,1,0:T(8,128)(2,1)S(1)}) custom-call(s32[32]{0:T(128)} %place_ref.7, bf16[128,512]{1,0:T(8,128)(2,1)} %refs_0_.1, bf16[128,512]{1,0:T(8,128)(2,1)} %refs_1_.2, f32[320,128]{1,0:T(8,128)} %constant.2.clone.refs_2_.rest_8_.rest_4_), custom_call_target="tpu_custom_call" | custom-call | flops 1000000000 | bytes 1048576 | tf_op jit(solution)/shard_map/rotate_keys/pallas_call | solution.py:90
  2.5 0.7 collective-permute-start
  3.2 3.0 %rotate_queries.1 = (bf16[2,2,8,128,128]{4,3,2,1,0:T(8,128)(2,1)S(1)}, bf16[2,2,8,128,128]{4,3,2,1,0:T(8,128)(2,1)S(1)}) custom-call(s32[32]{0:T(128)} %place_ref.7, bf16[128,4096]{1,0:T(8,128)(2,1)} %refs_0_.2, bf16[128,4096]{1,0:T(8,128)(2,1)} %refs_1_.3, f32[320,128]{1,0:T(8,128)} %constant.2.clone.refs_2_.rest_8_.rest_4_), custom_call_target="tpu_custom_call" | custom-call | flops 1000000000 | bytes 1048576 | tf_op jit(solution)/shard_map/rotate_queries/pallas_call | solution.py:90
  6.3 0.0 copy-start.1
  6.3 1.0 copy-done.1
  7.2 0.0 collective-permute-done
  7.2 0.0 collective-permute-start.1
  7.3 3.1 %collective-permute-start.4 = (bf16[2,2,2,128,128]{4,3,2,1,0:T(8,128)(2,1)S(1)}, bf16[2,2,2,128,128]{4,3,2,1,0:T(8,128)(2,1)S(1)}, u32[]{:S(2)}, u32[]{:S(2)}) collective-permute-start(bf16[2,2,2,128,128]{4,3,2,1,0:T(8,128)(2,1)S(1)} %pad_maximum_fusion.rest_0_.rest_4_), channel_id=1, source_target_pairs={{0,8},{8,16},{16,24},{1,9},{9,17},{17,25},{2,10},{10,18},{18,26},{... | collective-permute-start | bytes 786440 | tf_op jit(solution)/shard_map/ppermute | solution.py:453
  10.4 1.4 %collective-permute-start.2 = (bf16[2,2,2,128,128]{4,3,2,1,0:T(8,128)(2,1)S(1)}, bf16[2,2,2,128,128]{4,3,2,1,0:T(8,128)(2,1)S(1)}, u32[]{:S(2)}, u32[]{:S(2)}) collective-permute-start(bf16[2,2,2,128,128]{4,3,2,1,0:T(8,128)(2,1)S(1)} %pad_maximum_fusion.rest_0_.rest_4_), channel_id=1, source_target_pairs={{0,2},{1,3},{2,0},{3,1},{4,6},{5,7},{6,4},{7,5},{8,10},{9,11},{10,... | collective-permute-start | bytes 786440 | tf_op jit(solution)/shard_map/ppermute | solution.py:447
  11.8 2.3 %collective-permute-start.3 = (bf16[2,2,2,128,128]{4,3,2,1,0:T(8,128)(2,1)S(1)}, bf16[2,2,2,128,128]{4,3,2,1,0:T(8,128)(2,1)S(1)}, u32[]{:S(2)}, u32[]{:S(2)}) collective-permute-start(bf16[2,2,2,128,128]{4,3,2,1,0:T(8,128)(2,1)S(1)} %pad_maximum_fusion.rest_0_.rest_4_), channel_id=1, source_target_pairs={{0,4},{1,5},{2,6},{3,7},{4,0},{5,1},{6,2},{7,3},{8,12},{9,13},{10,... | collective-permute-start | bytes 786440 | tf_op jit(solution)/shard_map/ppermute | solution.py:447
  14.1 3.4 %collective-permute-done.4.rest_0_ = bf16[2,2,2,128,128]{4,3,2,1,0:T(8,128)(2,1)S(1)} collective-permute-done((bf16[2,2,2,128,128]{4,3,2,1,0:T(8,128)(2,1)S(1)}, bf16[2,2,2,128,128]{4,3,2,1,0:T(8,128)(2,1)S(1)}, u32[]{:S(2)}, u32[]{:S(2)}) %collective-permute-start.4) | collective-permute-done | bytes 262176 | tf_op jit(solution)/shard_map/ppermute | solution.py:453
  17.5 5.6 %collective-permute-done.2.rest_1_.rest_5_ = bf16[2,2,2,128,128]{4,3,2,1,0:T(8,128)(2,1)S(1)} collective-permute-done((bf16[2,2,2,128,128]{4,3,2,1,0:T(8,128)(2,1)S(1)}, bf16[2,2,2,128,128]{4,3,2,1,0:T(8,128)(2,1)S(1)}, u32[]{:S(2)}, u32[]{:S(2)}) %collective-permute-start.2) | collective-permute-done | bytes 262176 | tf_op jit(solution)/shard_map/ppermute | solution.py:447
  23.0 0.0 collective-permute-done.3.rest_2_.rest_6_
  23.0 1.9 %collective-permute-start.7 = (bf16[2,2,2,128,128]{4,3,2,1,0:T(8,128)(2,1)S(1)}, bf16[2,2,2,128,128]{4,3,2,1,0:T(8,128)(2,1)S(1)}, u32[]{:S(2)}, u32[]{:S(2)}) collective-permute-start(bf16[2,2,2,128,128]{4,3,2,1,0:T(8,128)(2,1)S(1)} %collective-permute-done.3.rest_2_.rest_6_), channel_id=1, source_target_pairs={{0,8},{8,16},{16,24},{1,9},{9,17},{17,25},{2,10},{10,18},{18,26},{... | collective-permute-start | bytes 786440 | tf_op jit(solution)/shard_map/ppermute | solution.py:453
  25.0 2.5 %collective-permute-start.5 = (bf16[2,2,2,128,128]{4,3,2,1,0:T(8,128)(2,1)S(1)}, bf16[2,2,2,128,128]{4,3,2,1,0:T(8,128)(2,1)}, u32[]{:S(2)}, u32[]{:S(2)}) collective-permute-start(bf16[2,2,2,128,128]{4,3,2,1,0:T(8,128)(2,1)S(1)} %collective-permute-done.3.rest_2_.rest_6_), channel_id=1, source_target_pairs={{0,2},{1,3},{2,0},{3,1},{4,6},{5,7},{6,4},{7,5},{8,10},{9,11},{10,... | collective-permute-start | bytes 786440 | tf_op jit(solution)/shard_map/ppermute | solution.py:447
  27.5 1.4 %copy.15.key_blocks = s32[32,12]{1,0:T(8,128)} copy(s32[32,12]{0,1:T(8,128)} %param.12) | data formatting | bytes 3072 | tf_op args[4]
  28.9 1.9 %collective-permute-start.6 = (bf16[2,2,2,128,128]{4,3,2,1,0:T(8,128)(2,1)S(1)}, bf16[2,2,2,128,128]{4,3,2,1,0:T(8,128)(2,1)S(1)}, u32[]{:S(2)}, u32[]{:S(2)}) collective-permute-start(bf16[2,2,2,128,128]{4,3,2,1,0:T(8,128)(2,1)S(1)} %collective-permute-done.2.rest_1_.rest_5_), channel_id=1, source_target_pairs={{0,8},{8,16},{16,24},{1,9},{9,17},{17,25},{2,10},{10,18},{18,26},{... | collective-permute-start | bytes 786440 | tf_op jit(solution)/shard_map/ppermute | solution.py:453
  30.8 0.3 collective-permute-done.7.rest_2_
  31.0 3.3 %collective-permute-start.8 = (bf16[2,2,2,128,128]{4,3,2,1,0:T(8,128)(2,1)S(1)}, bf16[2,2,2,128,128]{4,3,2,1,0:T(8,128)(2,1)S(1)}, u32[]{:S(2)}, u32[]{:S(2)}) collective-permute-start(bf16[2,2,2,128,128]{4,3,2,1,0:T(8,128)(2,1)S(1)} %collective-permute-done.7.rest_2_), channel_id=1, source_target_pairs={{0,2},{1,3},{2,0},{3,1},{4,6},{5,7},{6,4},{7,5},{8,10},{9,11},{10,... | collective-permute-start | bytes 786440 | tf_op jit(solution)/shard_map/ppermute | solution.py:447
  34.4 0.0 collective-permute-done.5.rest_3_.rest_7_
  34.4 0.0 collective-permute-done.1.other
  34.4 0.0 copy-start.2
  34.4 1.2 %copy-done.2 = bf16[2,2,8,128,128]{4,3,2,1,0:T(8,128)(2,1)S(1)} copy-done((bf16[2,2,8,128,128]{4,3,2,1,0:T(8,128)(2,1)S(1)}, bf16[2,2,8,128,128]{4,3,2,1,0:T(8,128)(2,1)}, u32[]{:S(2)}) %copy-start.2) | copy-done | bytes 1048600
  35.6 2.8 %current_statistics.1.stats_in = f32[2,2,8,1024]{3,2,1,0:T(8,128)S(1)} custom-call(s32[32,12]{1,0:T(8,128)} %copy.15.key_blocks, s32[32]{0:T(128)} %key_counts.9, bf16[2,2,8,128,128]{4,3,2,1,0:T(8,128)(2,1)S(1)} %copy-done.2, bf16[2,2,8,128,128]{4,3,2,1,0:T(8,128)(2,1)S(1)} %collective-permute-done.1.other, ...), custom_call_target="tpu_custom_call" | custom-call | flops 6000000000 | bytes 1048576 | tf_op jit(solution)/shard_map/current_statistics/pallas_call | solution.py:90
  38.4 1.7 %collective-permute-done.6.rest_1_ = bf16[2,2,2,128,128]{4,3,2,1,0:T(8,128)(2,1)S(1)} collective-permute-done((bf16[2,2,2,128,128]{4,3,2,1,0:T(8,128)(2,1)S(1)}, bf16[2,2,2,128,128]{4,3,2,1,0:T(8,128)(2,1)S(1)}, u32[]{:S(2)}, u32[]{:S(2)}) %collective-permute-start.6) | collective-permute-done | bytes 262176 | tf_op jit(solution)/shard_map/ppermute | solution.py:453
  40.0 0.0 collective-permute-done.8.rest_3_
  40.0 12.9 %previous_gradients.1 = (bf16[2,2,2,128,128]{4,3,2,1,0:T(8,128)(2,1)S(1)}, bf16[2,2,2,128,128]{4,3,2,1,0:T(8,128)(2,1)S(1)}, bf16[2,2,2,128,128]{4,3,2,1,0:T(8,1...) custom-call(s32[32,12]{1,0:T(8,128)} %copy.15.key_blocks, ...), custom_call_target="tpu_custom_call" | custom-call | flops 14000000000 | bytes 1048576 | tf_op jit(solution)/shard_map/previous_gradients/pallas_call | solution.py:90
  53.0 1.9 %collective-permute-start.9 = (bf16[2,2,2,128,128]{4,3,2,1,0:T(8,128)(2,1)S(1)}, bf16[2,2,2,128,128]{4,3,2,1,0:T(8,128)(2,1)S(1)}, u32[]{:S(2)}, u32[]{:S(2)}) collective-permute-start(bf16[2,2,2,128,128]{4,3,2,1,0:T(8,128)(2,1)S(1)} %get-tuple-element.60), channel_id=1, source_target_pairs={{8,0},{16,8},{24,16},{9,1},{17,9},{25,17},{10,2},{18,10},{26,18},{... | collective-permute-start | bytes 786440 | tf_op jit(solution)/shard_map/ppermute | solution.py:456
  54.9 0.1 collective-permute-start.10
  55.0 0.0 copy-start
  55.0 6.0 %current_gradients.1 = (f32[2,2,2,128,128]{4,3,2,1,0:T(8,128)S(1)}, f32[2,2,2,128,128]{4,3,2,1,0:T(8,128)S(1)}, f32[2,2,2,128,128]{4,3,2,1,0:T(8,128)S(1)}, bf16...) custom-call(s32[32,12]{1,0:T(8,128)} %copy.15.key_blocks, s32[32]{0:T(128)} %key_counts.9, ...), custom_call_target="tpu_custom_call" | custom-call | flops 10000000000 | bytes 1048576 | tf_op jit(solution)/shard_map/current_gradients/pallas_call | solution.py:90
  61.0 2.4 %collective-permute-start.12 = (bf16[2,2,2,128,128]{4,3,2,1,0:T(8,128)(2,1)S(1)}, bf16[2,2,2,128,128]{4,3,2,1,0:T(8,128)(2,1)S(1)}, u32[]{:S(2)}, u32[]{:S(2)}) collective-permute-start(bf16[2,2,2,128,128]{4,3,2,1,0:T(8,128)(2,1)S(1)} %get-tuple-element.73), channel_id=1, source_target_pairs={{0,2},{1,3},{2,0},{3,1},{4,6},{5,7},{6,4},{7,5},{8,10},{9,11},{10,... | collective-permute-start | bytes 786440 | tf_op jit(solution)/shard_map/ppermute | solution.py:447
  63.4 0.0 collective-permute-done.9
  63.4 0.1 add_convert_fusion.2
  63.5 0.1 collective-permute-start.16
  63.6 0.0 collective-permute-done.10
  63.6 0.1 add_convert_fusion.1
  63.6 1.9 %collective-permute-start.11 = (bf16[2,2,2,128,128]{4,3,2,1,0:T(8,128)(2,1)S(1)}, bf16[2,2,2,128,128]{4,3,2,1,0:T(8,128)(2,1)S(1)}, u32[]{:S(2)}, u32[]{:S(2)}) collective-permute-start(bf16[2,2,2,128,128]{4,3,2,1,0:T(8,128)(2,1)S(1)} %add_convert_fusion.1), channel_id=1, source_target_pairs={{8,0},{16,8},{24,16},{9,1},{17,9},{25,17},{10,2},{18,10},{26,18},{... | collective-permute-start | bytes 786440 | tf_op jit(solution)/shard_map/ppermute | solution.py:456
  65.6 1.9 %collective-permute-start.15 = (bf16[2,2,2,128,128]{4,3,2,1,0:T(8,128)(2,1)S(1)}, bf16[2,2,2,128,128]{4,3,2,1,0:T(8,128)(2,1)S(1)}, u32[]{:S(2)}, u32[]{:S(2)}) collective-permute-start(bf16[2,2,2,128,128]{4,3,2,1,0:T(8,128)(2,1)S(1)} %get-tuple-element.81), channel_id=1, source_target_pairs={{8,0},{16,8},{24,16},{9,1},{17,9},{25,17},{10,2},{18,10},{26,18},{... | collective-permute-start | bytes 786440 | tf_op jit(solution)/shard_map/ppermute | solution.py:456
  67.5 0.0 copy-done
  67.5 5.7 %query_results.2 = (bf16[2,128,1024]{2,1,0:T(8,128)(2,1)S(1)}, bf16[2,128,1024]{2,1,0:T(8,128)(2,1)S(1)}) custom-call(s32[32,12]{1,0:T(8,128)} %copy.15.key_blocks, s32[32]{0:T(128)} %key_counts.9, s32[32]{0:T(128)} %place_ref.7, bf16[2,8,2,2,128,1024]{5,4,3,2,1,0:T(8,128)(2,1)} %get-tuple-element.62.far_saved, ...), custom_call_target="tpu_custom_call" | custom-call | flops 20000000000 | bytes 1048576 | tf_op jit(solution)/shard_map/query_results/pallas_call | solution.py:90
  73.2 4.3 %collective-permute-start.13 = (bf16[2,128,1024]{2,1,0:T(8,128)(2,1)S(1)}, bf16[2,128,1024]{2,1,0:T(8,128)(2,1)S(1)}, u32[]{:S(2)}, u32[]{:S(2)}) collective-permute-start(bf16[2,128,1024]{2,1,0:T(8,128)(2,1)S(1)} %get-tuple-element.67), channel_id=1, source_target_pairs={{0,1},{1,0},{2,3},{3,2},{4,5},{5,4},{6,7},{7,6},{8,9},{9,8},{10,11... | collective-permute-start | bytes 1572872 | tf_op jit(solution)/shard_map/ppermute | solution.py:447
  77.5 0.0 collective-permute-done.12
  77.5 0.0 collective-permute-done.11
  77.5 0.1 add_convert_fusion
  77.6 9.9 %collective-permute-start.17 = (bf16[2,2,2,128,128]{4,3,2,1,0:T(8,128)(2,1)S(1)}, bf16[2,2,2,128,128]{4,3,2,1,0:T(8,128)(2,1)S(1)}, u32[]{:S(2)}, u32[]{:S(2)}) collective-permute-start(bf16[2,2,2,128,128]{4,3,2,1,0:T(8,128)(2,1)S(1)} %add_convert_fusion), channel_id=1, source_target_pairs={{0,4},{1,5},{2,6},{3,7},{4,0},{5,1},{6,2},{7,3},{8,12},{9,13},{10,... | collective-permute-start | bytes 786440 | tf_op jit(solution)/shard_map/ppermute | solution.py:447
  87.6 5.7 %query_results.3 = (bf16[2,128,1024]{2,1,0:T(8,128)(2,1)S(1)}, bf16[2,128,1024]{2,1,0:T(8,128)(2,1)S(1)}) custom-call(s32[32,12]{1,0:T(8,128)} %copy.15.key_blocks, s32[32]{0:T(128)} %key_counts.9, s32[32]{0:T(128)} %place_ref.7, bf16[2,8,2,2,128,1024]{5,4,3,2,1,0:T(8,128)(2,1)} %get-tuple-element.62.far_saved, ...), custom_call_target="tpu_custom_call" | custom-call | flops 20000000000 | bytes 1048576 | tf_op jit(solution)/shard_map/query_results/pallas_call | solution.py:90
  93.2 0.3 collective-permute-start.14
  93.6 0.0 collective-permute-done.15.rest_1_
  93.6 0.0 collective-permute-done.16.rest_2_
  93.6 6.3 %collective-permute-done.17.rest_3_ = bf16[2,2,2,128,128]{4,3,2,1,0:T(8,128)(2,1)S(1)} collective-permute-done((bf16[2,2,2,128,128]{4,3,2,1,0:T(8,128)(2,1)S(1)}, bf16[2,2,2,128,128]{4,3,2,1,0:T(8,128)(2,1)S(1)}, u32[]{:S(2)}, u32[]{:S(2)}) %collective-permute-start.17) | collective-permute-done | bytes 262176 | tf_op jit(solution)/shard_map/ppermute | solution.py:447
  99.8 0.9 key_gradients.1
  100.7 0.5 collective-permute-start.18
  101.2 1.0 collective-permute-done.18.refs_1_
  102.2 0.7 join_keys.1
  102.9 0.0 collective-permute-done.13.refs_2_
  102.9 0.0 collective-permute-done.14.refs_3_
  102.9 1.5 %join_queries.1 = (bf16[128,4096]{1,0:T(8,128)(2,1)}, bf16[128,4096]{1,0:T(8,128)(2,1)}) custom-call(bf16[2,128,1024]{2,1,0:T(8,128)(2,1)S(1)} %get-tuple-element.64.refs_0_, bf16[2,128,1024]{2,1,0:T(8,128)(2,1)S(1)} %get-tuple-element.76.refs_1_, bf16[2,128,1024]{2,1,0:T(8,128)(2,1)S(1)} %collective-permute-done.13.refs_2_, ...), custom_call_target="tpu_custom_call" | custom-call | flops 2000000000 | bytes 1048576 | tf_op jit(solution)/shard_map/join_queries/pallas_call | solution.py:90
  (1 shorter events, 0.0 us)
Async XLA Ops:
  2.5 4.7 %collective-permute-start = (bf16[2,2,128,128]{3,2,1,0:T(8,128)(2,1)S(1)}, bf16[2,2,128,128]{3,2,1,0:T(8,128)(2,1)S(1)}, u32[]{:S(2)}, u32[]{:S(2)}) collective-permute-start(bf16[2,2,128,128]{3,2,1,0:T(8,128)(2,1)S(1)} %get-tuple-element.49), channel_id=1, source_target_pairs={{0,1},{1,0},{2,3},{3,2},{4,5},{5,4},{6,7},{7,6},{8,9},{9,8},{10,11... | collective-permute-start | bytes 393224 | tf_op jit(solution)/shard_map/ppermute | solution.py:447
  6.3 1.0 copy-start.1
  7.2 27.1 %collective-permute-start.1 = (bf16[2,2,8,128,128]{4,3,2,1,0:T(8,128)(2,1)S(1)}, bf16[2,2,8,128,128]{4,3,2,1,0:T(8,128)(2,1)S(1)}, u32[]{:S(2)}, u32[]{:S(2)}) collective-permute-start(bf16[2,2,8,128,128]{4,3,2,1,0:T(8,128)(2,1)S(1)} %get-tuple-element.52), channel_id=1, source_target_pairs={{0,1},{1,0},{2,3},{3,2},{4,5},{5,4},{6,7},{7,6},{8,9},{9,8},{10,11... | collective-permute-start | bytes 3145736 | tf_op jit(solution)/shard_map/ppermute | solution.py:447
  7.3 10.2 %collective-permute-start.4 = (bf16[2,2,2,128,128]{4,3,2,1,0:T(8,128)(2,1)S(1)}, bf16[2,2,2,128,128]{4,3,2,1,0:T(8,128)(2,1)S(1)}, u32[]{:S(2)}, u32[]{:S(2)}) collective-permute-start(bf16[2,2,2,128,128]{4,3,2,1,0:T(8,128)(2,1)S(1)} %pad_maximum_fusion.rest_0_.rest_4_), channel_id=1, source_target_pairs={{0,8},{8,16},{16,24},{1,9},{9,17},{17,25},{2,10},{10,18},{18,26},{... | collective-permute-start | bytes 786440 | tf_op jit(solution)/shard_map/ppermute | solution.py:453
  10.4 12.6 %collective-permute-start.2 = (bf16[2,2,2,128,128]{4,3,2,1,0:T(8,128)(2,1)S(1)}, bf16[2,2,2,128,128]{4,3,2,1,0:T(8,128)(2,1)S(1)}, u32[]{:S(2)}, u32[]{:S(2)}) collective-permute-start(bf16[2,2,2,128,128]{4,3,2,1,0:T(8,128)(2,1)S(1)} %pad_maximum_fusion.rest_0_.rest_4_), channel_id=1, source_target_pairs={{0,2},{1,3},{2,0},{3,1},{4,6},{5,7},{6,4},{7,5},{8,10},{9,11},{10,... | collective-permute-start | bytes 786440 | tf_op jit(solution)/shard_map/ppermute | solution.py:447
  11.8 11.3 %collective-permute-start.3 = (bf16[2,2,2,128,128]{4,3,2,1,0:T(8,128)(2,1)S(1)}, bf16[2,2,2,128,128]{4,3,2,1,0:T(8,128)(2,1)S(1)}, u32[]{:S(2)}, u32[]{:S(2)}) collective-permute-start(bf16[2,2,2,128,128]{4,3,2,1,0:T(8,128)(2,1)S(1)} %pad_maximum_fusion.rest_0_.rest_4_), channel_id=1, source_target_pairs={{0,4},{1,5},{2,6},{3,7},{4,0},{5,1},{6,2},{7,3},{8,12},{9,13},{10,... | collective-permute-start | bytes 786440 | tf_op jit(solution)/shard_map/ppermute | solution.py:447
  23.0 8.0 %collective-permute-start.7 = (bf16[2,2,2,128,128]{4,3,2,1,0:T(8,128)(2,1)S(1)}, bf16[2,2,2,128,128]{4,3,2,1,0:T(8,128)(2,1)S(1)}, u32[]{:S(2)}, u32[]{:S(2)}) collective-permute-start(bf16[2,2,2,128,128]{4,3,2,1,0:T(8,128)(2,1)S(1)} %collective-permute-done.3.rest_2_.rest_6_), channel_id=1, source_target_pairs={{0,8},{8,16},{16,24},{1,9},{9,17},{17,25},{2,10},{10,18},{18,26},{... | collective-permute-start | bytes 786440 | tf_op jit(solution)/shard_map/ppermute | solution.py:453
  25.0 9.4 %collective-permute-start.5 = (bf16[2,2,2,128,128]{4,3,2,1,0:T(8,128)(2,1)S(1)}, bf16[2,2,2,128,128]{4,3,2,1,0:T(8,128)(2,1)}, u32[]{:S(2)}, u32[]{:S(2)}) collective-permute-start(bf16[2,2,2,128,128]{4,3,2,1,0:T(8,128)(2,1)S(1)} %collective-permute-done.3.rest_2_.rest_6_), channel_id=1, source_target_pairs={{0,2},{1,3},{2,0},{3,1},{4,6},{5,7},{6,4},{7,5},{8,10},{9,11},{10,... | collective-permute-start | bytes 786440 | tf_op jit(solution)/shard_map/ppermute | solution.py:447
  28.9 11.2 %collective-permute-start.6 = (bf16[2,2,2,128,128]{4,3,2,1,0:T(8,128)(2,1)S(1)}, bf16[2,2,2,128,128]{4,3,2,1,0:T(8,128)(2,1)S(1)}, u32[]{:S(2)}, u32[]{:S(2)}) collective-permute-start(bf16[2,2,2,128,128]{4,3,2,1,0:T(8,128)(2,1)S(1)} %collective-permute-done.2.rest_1_.rest_5_), channel_id=1, source_target_pairs={{0,8},{8,16},{16,24},{1,9},{9,17},{17,25},{2,10},{10,18},{18,26},{... | collective-permute-start | bytes 786440 | tf_op jit(solution)/shard_map/ppermute | solution.py:453
  31.0 9.0 %collective-permute-start.8 = (bf16[2,2,2,128,128]{4,3,2,1,0:T(8,128)(2,1)S(1)}, bf16[2,2,2,128,128]{4,3,2,1,0:T(8,128)(2,1)S(1)}, u32[]{:S(2)}, u32[]{:S(2)}) collective-permute-start(bf16[2,2,2,128,128]{4,3,2,1,0:T(8,128)(2,1)S(1)} %collective-permute-done.7.rest_2_), channel_id=1, source_target_pairs={{0,2},{1,3},{2,0},{3,1},{4,6},{5,7},{6,4},{7,5},{8,10},{9,11},{10,... | collective-permute-start | bytes 786440 | tf_op jit(solution)/shard_map/ppermute | solution.py:447
  34.4 1.2 %copy-start.2 = (bf16[2,2,8,128,128]{4,3,2,1,0:T(8,128)(2,1)S(1)}, bf16[2,2,8,128,128]{4,3,2,1,0:T(8,128)(2,1)}, u32[]{:S(2)}) copy-start(bf16[2,2,8,128,128]{4,3,2,1,0:T(8,128)(2,1)} %copy-done.1) | copy-start | bytes 3145732
  53.0 10.4 %collective-permute-start.9 = (bf16[2,2,2,128,128]{4,3,2,1,0:T(8,128)(2,1)S(1)}, bf16[2,2,2,128,128]{4,3,2,1,0:T(8,128)(2,1)S(1)}, u32[]{:S(2)}, u32[]{:S(2)}) collective-permute-start(bf16[2,2,2,128,128]{4,3,2,1,0:T(8,128)(2,1)S(1)} %get-tuple-element.60), channel_id=1, source_target_pairs={{8,0},{16,8},{24,16},{9,1},{17,9},{25,17},{10,2},{18,10},{26,18},{... | collective-permute-start | bytes 786440 | tf_op jit(solution)/shard_map/ppermute | solution.py:456
  54.9 8.7 %collective-permute-start.10 = (bf16[2,2,2,128,128]{4,3,2,1,0:T(8,128)(2,1)S(1)}, bf16[2,2,2,128,128]{4,3,2,1,0:T(8,128)(2,1)S(1)}, u32[]{:S(2)}, u32[]{:S(2)}) collective-permute-start(bf16[2,2,2,128,128]{4,3,2,1,0:T(8,128)(2,1)S(1)} %get-tuple-element.71), channel_id=1, source_target_pairs={{0,2},{1,3},{2,0},{3,1},{4,6},{5,7},{6,4},{7,5},{8,10},{9,11},{10,... | collective-permute-start | bytes 786440 | tf_op jit(solution)/shard_map/ppermute | solution.py:447
  55.0 12.5 %copy-start = (f32[320,128]{1,0:T(8,128)S(1)}, f32[320,128]{1,0:T(8,128)}, u32[]{:S(2)}) copy-start(f32[320,128]{1,0:T(8,128)} %constant.2.clone.refs_2_.rest_8_.rest_4_) | copy-start | bytes 491524
  61.0 16.5 %collective-permute-start.12 = (bf16[2,2,2,128,128]{4,3,2,1,0:T(8,128)(2,1)S(1)}, bf16[2,2,2,128,128]{4,3,2,1,0:T(8,128)(2,1)S(1)}, u32[]{:S(2)}, u32[]{:S(2)}) collective-permute-start(bf16[2,2,2,128,128]{4,3,2,1,0:T(8,128)(2,1)S(1)} %get-tuple-element.73), channel_id=1, source_target_pairs={{0,2},{1,3},{2,0},{3,1},{4,6},{5,7},{6,4},{7,5},{8,10},{9,11},{10,... | collective-permute-start | bytes 786440 | tf_op jit(solution)/shard_map/ppermute | solution.py:447
  63.5 30.1 %collective-permute-start.16 = (bf16[2,2,2,128,128]{4,3,2,1,0:T(8,128)(2,1)S(1)}, bf16[2,2,2,128,128]{4,3,2,1,0:T(8,128)(2,1)S(1)}, u32[]{:S(2)}, u32[]{:S(2)}) collective-permute-start(bf16[2,2,2,128,128]{4,3,2,1,0:T(8,128)(2,1)S(1)} %add_convert_fusion.2), channel_id=1, source_target_pairs={{0,2},{1,3},{2,0},{3,1},{4,6},{5,7},{6,4},{7,5},{8,10},{9,11},{10,... | collective-permute-start | bytes 786440 | tf_op jit(solution)/shard_map/ppermute | solution.py:447
  63.6 13.9 %collective-permute-start.11 = (bf16[2,2,2,128,128]{4,3,2,1,0:T(8,128)(2,1)S(1)}, bf16[2,2,2,128,128]{4,3,2,1,0:T(8,128)(2,1)S(1)}, u32[]{:S(2)}, u32[]{:S(2)}) collective-permute-start(bf16[2,2,2,128,128]{4,3,2,1,0:T(8,128)(2,1)S(1)} %add_convert_fusion.1), channel_id=1, source_target_pairs={{8,0},{16,8},{24,16},{9,1},{17,9},{25,17},{10,2},{18,10},{26,18},{... | collective-permute-start | bytes 786440 | tf_op jit(solution)/shard_map/ppermute | solution.py:456
  65.6 28.0 %collective-permute-start.15 = (bf16[2,2,2,128,128]{4,3,2,1,0:T(8,128)(2,1)S(1)}, bf16[2,2,2,128,128]{4,3,2,1,0:T(8,128)(2,1)S(1)}, u32[]{:S(2)}, u32[]{:S(2)}) collective-permute-start(bf16[2,2,2,128,128]{4,3,2,1,0:T(8,128)(2,1)S(1)} %get-tuple-element.81), channel_id=1, source_target_pairs={{8,0},{16,8},{24,16},{9,1},{17,9},{25,17},{10,2},{18,10},{26,18},{... | collective-permute-start | bytes 786440 | tf_op jit(solution)/shard_map/ppermute | solution.py:456
  73.2 29.7 %collective-permute-start.13 = (bf16[2,128,1024]{2,1,0:T(8,128)(2,1)S(1)}, bf16[2,128,1024]{2,1,0:T(8,128)(2,1)S(1)}, u32[]{:S(2)}, u32[]{:S(2)}) collective-permute-start(bf16[2,128,1024]{2,1,0:T(8,128)(2,1)S(1)} %get-tuple-element.67), channel_id=1, source_target_pairs={{0,1},{1,0},{2,3},{3,2},{4,5},{5,4},{6,7},{7,6},{8,9},{9,8},{10,11... | collective-permute-start | bytes 1572872 | tf_op jit(solution)/shard_map/ppermute | solution.py:447
  77.6 22.2 %collective-permute-start.17 = (bf16[2,2,2,128,128]{4,3,2,1,0:T(8,128)(2,1)S(1)}, bf16[2,2,2,128,128]{4,3,2,1,0:T(8,128)(2,1)S(1)}, u32[]{:S(2)}, u32[]{:S(2)}) collective-permute-start(bf16[2,2,2,128,128]{4,3,2,1,0:T(8,128)(2,1)S(1)} %add_convert_fusion), channel_id=1, source_target_pairs={{0,4},{1,5},{2,6},{3,7},{4,0},{5,1},{6,2},{7,3},{8,12},{9,13},{10,... | collective-permute-start | bytes 786440 | tf_op jit(solution)/shard_map/ppermute | solution.py:447
  93.2 9.6 %collective-permute-start.14 = (bf16[2,128,1024]{2,1,0:T(8,128)(2,1)S(1)}, bf16[2,128,1024]{2,1,0:T(8,128)(2,1)S(1)}, u32[]{:S(2)}, u32[]{:S(2)}) collective-permute-start(bf16[2,128,1024]{2,1,0:T(8,128)(2,1)S(1)} %get-tuple-element.77), channel_id=1, source_target_pairs={{0,1},{1,0},{2,3},{3,2},{4,5},{5,4},{6,7},{7,6},{8,9},{9,8},{10,11... | collective-permute-start | bytes 1572872 | tf_op jit(solution)/shard_map/ppermute | solution.py:447
  100.7 1.5 %collective-permute-start.18 = (bf16[2,128,256]{2,1,0:T(8,128)(2,1)S(1)}, bf16[2,128,256]{2,1,0:T(8,128)(2,1)S(1)}, u32[]{:S(2)}, u32[]{:S(2)}) collective-permute-start(bf16[2,128,256]{2,1,0:T(8,128)(2,1)S(1)} %get-tuple-element.83), channel_id=1, source_target_pairs={{0,1},{1,0},{2,3},{3,2},{4,5},{5,4},{6,7},{7,6},{8,9},{9,8},{10,11... | collective-permute-start | bytes 393224 | tf_op jit(solution)/shard_map/ppermute | solution.py:447
where the time goes:
time: 105 us; the launch traced here: 104 us
  Pallas kernels  41 us (39%)
  starting transfers between devices  40.6 us (39%)
  waiting for transfers between devices  18.2 us (17%)
  local copies, waits for them, and re-layouts  3.57 us (3%)
    pallas_call x10, Pallas kernels, run(): pl.pallas_call(kernel, out_shape=[pltpu.HBM(a.shape, a.dtype) if n == hbm...  41 us
    ppermute x13, starting transfers between devices, cross(): return lax.ppermute(array, 'seq', [(m, m ^ by) for m in range(n_seq)])  27.9 us
    ppermute x13, waiting for transfers between devices, cross(): return lax.ppermute(array, 'seq', [(m, m ^ by) for m in range(n_seq)])  12.9 us
    ppermute x3, starting transfers between devices, onward(): return lax.ppermute(array, 'grp', [(g, g + 1) for g in range(n_grp - 1)])  6.94 us
    ppermute x3, starting transfers between devices, back(): return lax.ppermute(array, 'grp', [(g + 1, g) for g in range(n_grp - 1)])  5.76 us
    ppermute x3, waiting for transfers between devices, onward(): return lax.ppermute(array, 'grp', [(g, g + 1) for g in range(n_grp - 1)])  5.29 us
    unnamed x7, local copies, waits for them, and re-layouts  3.57 us
  transfers between devices with their start and end apart: 19, of which 6 were waited for; matrix products, arithmetic and copies ran while one was open for 2% of the time, Pallas kernels for 24%

commit v1 on v0

--- a/solution.py
+++ b/solution.py
@@ -184,17 +184,17 @@
         store[first + CORES * k : first + CORES * (k + 1)] = piece[...]
 
 
-def pair_scores(store, e, h, block, rows, diagonal):
-    scores = dot_nt(store[e, 0, h], heads_of(block, 0, h, rows))
+def pair_scores(store, e, h, turned, i, columns, diagonal):
+    scores = dot_nn(store[e, 0, h], turned[i, 0, h, :, columns])
     if diagonal:
         scores = jnp.where(causal(), scores, -1e30)
-    return scores, dot_nt(store[e, 1, h], heads_of(block, 1, h, rows))
-
-
-def gather_stats(store, e, block, stats, i, diagonal, kept=None):
+    return scores, dot_nn(store[e, 1, h], turned[i, 1, h, :, columns])
+
+
+def gather_stats(store, e, turned, stats, i, diagonal, kept=None):
     for h in range(HALF_KV):
-        for rows, columns in chunks():
-            scores, dprobs = pair_scores(store, e, h, block, rows, diagonal)
+        for _, columns in chunks():
+            scores, dprobs = pair_scores(store, e, h, turned, i, columns, diagonal)
             if kept is not None:
                 n, kept_scores, kept_dprobs = kept
                 kept_scores[n, h, :, columns] = scores
@@ -255,24 +255,28 @@
 
 def current_stats(n_seq, key_blocks, key_counts, own, other, *rest):
     n_pieces = n_seq // CORES
-    pieces, (stats, store, found) = rest[:n_pieces], rest[n_pieces:]
+    pieces, (turned, stats, store, found) = rest[:n_pieces], rest[n_pieces:]
     group, member, _ = here(n_seq)
     fill(store, pieces)
     for i, block in enumerate((own, other)):
-        gather_stats(store, i, block, stats, i, True)
+        for w in range(2):
+            for h in range(HALF_KV):
+                for r in range(RATIO):
+                    turned[i, w, h, :, r * BLK : (r + 1) * BLK] = block[w, h, r].T
+        gather_stats(store, i, turned, stats, i, True)
         count = list_blocks(
             n_seq, 1, group * n_seq + lax.bitwise_xor(member, i), group, member,
             key_blocks, key_counts, found,
         )
 
         def step(n, _):
-            gather_stats(store, found[n], block, stats, i, False)
+            gather_stats(store, found[n], turned, stats, i, False)
             return 0
 
         lax.fori_loop(0, count, step, 0)
 
 
-def previous_grads(n_seq, key_blocks, key_counts, own, other, stats_in, *rest):
+def previous_grads(n_seq, key_blocks, key_counts, own, other, turned, stats_in, *rest):
     n_pieces = n_seq // CORES
     pieces, outs = rest[:n_pieces], rest[n_pieces : 2 * n_pieces]
     saved, stats, store, found, kept_scores, kept_dprobs, acc, low, sent = rest[2 * n_pieces :]
@@ -287,7 +291,7 @@
         )
 
         def look(n, _):
-            gather_stats(store, found[n], block, stats, i, False, (n, kept_scores, kept_dprobs))
+            gather_stats(store, found[n], turned, stats, i, False, (n, kept_scores, kept_dprobs))
             return 0
 
         lax.fori_loop(0, count, look, 0)
@@ -302,7 +306,7 @@
     write_grads(acc, outs)
 
 
-def current_grads(n_seq, key_blocks, key_counts, own, other, stats, *rest):
+def current_grads(n_seq, key_blocks, key_counts, own, other, turned, stats, *rest):
     n_pieces = n_seq // CORES
     pieces, outs = rest[:n_pieces], rest[n_pieces : 2 * n_pieces]
     saved, store, found, kept_scores, kept_dprobs, acc, low, sent = rest[2 * n_pieces :]
@@ -318,8 +322,10 @@
 
         def look(n, diagonal):
             for h in range(HALF_KV):
-                for rows, columns in chunks():
-                    scores, dprobs = pair_scores(store, found[n], h, block, rows, diagonal)
+                for _, columns in chunks():
+                    scores, dprobs = pair_scores(
+                        store, found[n], h, turned, i, columns, diagonal
+                    )
                     kept_scores[n, h, :, columns] = scores
                     kept_dprobs[n, h, :, columns] = dprobs
             return 0
@@ -482,18 +488,20 @@
     q_send, q_keep, kv_got, kv_keep = lax.optimization_barrier((q_send, q_keep, kv_got, kv_keep))
     q_got = cross(q_send, 1)
     near = [jnp.stack([kv_keep, kv_got])]
-    near += [along(near[0], 1)]
+    near.append(along(near[0], 1))
     ready, first_far = lax.optimization_barrier((near[1], onward(near[0])))
-    far = [first_far, onward(ready)]
+    far = [first_far, None]
     for k in range(2, n_pieces, 2):
         piece_k, _ = lax.optimization_barrier((along(near[0], k), ready))
-        near.append(piece_k)
-        far.append(onward(near[k]))
-        near.append(along(near[k], 1))
+        near += [piece_k, along(piece_k, 1)]
+        far.append(onward(piece_k))
         far.append(along(far[k], 1))
-
-    stats = call(
-        functools.partial(current_stats, n_seq), stats_shape, 2, [store, found],
+    ready, far[2] = lax.optimization_barrier((ready, far[2]))
+    far[1] = onward(ready)
+
+    turned_shape = jax.ShapeDtypeStruct((2, 2, HALF_KV, HEAD_DIM, ROWS), BF16)
+    turned, stats = call(
+        functools.partial(current_stats, n_seq), (turned_shape, stats_shape), 2, [store, found],
         us=6, name="current_statistics",
     )(key_blocks, key_counts, q_keep, q_got, *near)
 
@@ -512,11 +520,11 @@
 
     *far_grads, far_saved, stats = grads_call(
         previous_grads, n_far, (low,) * n_pieces + (stats_shape,), 14, "previous_gradients"
-    )(key_blocks, key_counts, q_keep, q_got, stats, *far)
+    )(key_blocks, key_counts, q_keep, q_got, turned, stats, *far)
     *near_grads, near_saved = grads_call(
         current_grads, min(n_seq, n_listed),
         tuple(low if k % 2 and k > 1 else high for k in range(n_pieces)), 10, "current_gradients",
-    )(key_blocks, key_counts, q_keep, q_got, stats, *near)
+    )(key_blocks, key_counts, q_keep, q_got, turned, stats, *near)
 
     half_out = jax.ShapeDtypeStruct((2, BLK, RATIO * HEAD_DIM), BF16)
 

time: 105 us -> 102 us (0.971)
  the two profiles are of different devices: /device:TPU:5 before, /device:TPU:7 now
where the time goes in v1:
time: 102 us; the launch traced here: 103 us
  Pallas kernels  47.9 us (47%)
  starting transfers between devices  32 us (31%)
  waiting for transfers between devices  18 us (18%)
  local copies, waits for them, and re-layouts  3.58 us (4%)
    pallas_call x10, Pallas kernels, run(): pl.pallas_call(kernel, out_shape=[pltpu.HBM(a.shape, a.dtype) if n == hbm...  47.9 us
    ppermute x13, starting transfers between devices, cross(): return lax.ppermute(array, 'seq', [(m, m ^ by) for m in range(n_seq)])  24.2 us
    ppermute x13, waiting for transfers between devices, cross(): return lax.ppermute(array, 'seq', [(m, m ^ by) for m in range(n_seq)])  11.5 us
    ppermute x3, waiting for transfers between devices, onward(): return lax.ppermute(array, 'grp', [(g, g + 1) for g in range(n_grp - 1)])  6.53 us
    ppermute x3, starting transfers between devices, back(): return lax.ppermute(array, 'grp', [(g + 1, g) for g in range(n_grp - 1)])  3.92 us
    ppermute x3, starting transfers between devices, onward(): return lax.ppermute(array, 'grp', [(g, g + 1) for g in range(n_grp - 1)])  3.85 us
    unnamed x9, local copies, waits for them, and re-layouts  3.58 us
  transfers between devices with their start and end apart: 19, of which 5 were waited for; matrix products, arithmetic and copies ran while one was open for 2% of the time, Pallas kernels for 26%

profile of v1, /device:TPU:7, one launch (start us, length us, event | category | flops | bytes accessed | tf_op | source)
XLA Modules:
  0.0 102.6 jit_solution(11523692702981927929)
XLA Ops:
  0.6 1.9 %rotate_keys.1 = (bf16[2,2,128,128]{3,2,1,0:T(8,128)(2,1)S(1)}, bf16[2,2,128,128]{3,2,1,0:T(8,128)(2,1)S(1)}) custom-call(s32[32]{0:T(128)} %place_ref.7, bf16[128,512]{1,0:T(8,128)(2,1)} %refs_0_.1, bf16[128,512]{1,0:T(8,128)(2,1)} %refs_1_.2, f32[320,128]{1,0:T(8,128)} %constant.2.clone.refs_2_.rest_8_.rest_4_), custom_call_target="tpu_custom_call" | custom-call | flops 1000000000 | bytes 1048576 | tf_op jit(solution)/shard_map/rotate_keys/pallas_call | solution.py:90
  2.5 0.7 collective-permute-start
  3.2 3.0 %rotate_queries.1 = (bf16[2,2,8,128,128]{4,3,2,1,0:T(8,128)(2,1)S(1)}, bf16[2,2,8,128,128]{4,3,2,1,0:T(8,128)(2,1)S(1)}) custom-call(s32[32]{0:T(128)} %place_ref.7, bf16[128,4096]{1,0:T(8,128)(2,1)} %refs_0_.2, bf16[128,4096]{1,0:T(8,128)(2,1)} %refs_1_.3, f32[320,128]{1,0:T(8,128)} %constant.2.clone.refs_2_.rest_8_.rest_4_), custom_call_target="tpu_custom_call" | custom-call | flops 1000000000 | bytes 1048576 | tf_op jit(solution)/shard_map/rotate_queries/pallas_call | solution.py:90
  6.3 0.0 copy-start.1
  6.3 1.0 copy-done.1
  7.2 0.0 collective-permute-done
  7.2 0.0 collective-permute-start.1
  7.3 1.3 %collective-permute-start.4 = (bf16[2,2,2,128,128]{4,3,2,1,0:T(8,128)(2,1)S(1)}, bf16[2,2,2,128,128]{4,3,2,1,0:T(8,128)(2,1)S(1)}, u32[]{:S(2)}, u32[]{:S(2)}) collective-permute-start(bf16[2,2,2,128,128]{4,3,2,1,0:T(8,128)(2,1)S(1)} %pad_maximum_fusion.rest_0_.rest_4_), channel_id=1, source_target_pairs={{0,8},{8,16},{16,24},{1,9},{9,17},{17,25},{2,10},{10,18},{18,26},{... | collective-permute-start | bytes 786440 | tf_op jit(solution)/shard_map/ppermute | solution.py:459
  8.6 1.4 %collective-permute-start.2 = (bf16[2,2,2,128,128]{4,3,2,1,0:T(8,128)(2,1)S(1)}, bf16[2,2,2,128,128]{4,3,2,1,0:T(8,128)(2,1)S(1)}, u32[]{:S(2)}, u32[]{:S(2)}) collective-permute-start(bf16[2,2,2,128,128]{4,3,2,1,0:T(8,128)(2,1)S(1)} %pad_maximum_fusion.rest_0_.rest_4_), channel_id=1, source_target_pairs={{0,2},{1,3},{2,0},{3,1},{4,6},{5,7},{6,4},{7,5},{8,10},{9,11},{10,... | collective-permute-start | bytes 786440 | tf_op jit(solution)/shard_map/ppermute | solution.py:453
  9.9 2.3 %collective-permute-start.3 = (bf16[2,2,2,128,128]{4,3,2,1,0:T(8,128)(2,1)S(1)}, bf16[2,2,2,128,128]{4,3,2,1,0:T(8,128)(2,1)S(1)}, u32[]{:S(2)}, u32[]{:S(2)}) collective-permute-start(bf16[2,2,2,128,128]{4,3,2,1,0:T(8,128)(2,1)S(1)} %pad_maximum_fusion.rest_0_.rest_4_), channel_id=1, source_target_pairs={{0,4},{1,5},{2,6},{3,7},{4,0},{5,1},{6,2},{7,3},{8,12},{9,13},{10,... | collective-permute-start | bytes 786440 | tf_op jit(solution)/shard_map/ppermute | solution.py:453
  12.3 4.3 %collective-permute-done.4.rest_0_ = bf16[2,2,2,128,128]{4,3,2,1,0:T(8,128)(2,1)S(1)} collective-permute-done((bf16[2,2,2,128,128]{4,3,2,1,0:T(8,128)(2,1)S(1)}, bf16[2,2,2,128,128]{4,3,2,1,0:T(8,128)(2,1)S(1)}, u32[]{:S(2)}, u32[]{:S(2)}) %collective-permute-start.4) | collective-permute-done | bytes 262176 | tf_op jit(solution)/shard_map/ppermute | solution.py:459
  16.6 5.0 %collective-permute-done.2.rest_1_.rest_5_ = bf16[2,2,2,128,128]{4,3,2,1,0:T(8,128)(2,1)S(1)} collective-permute-done((bf16[2,2,2,128,128]{4,3,2,1,0:T(8,128)(2,1)S(1)}, bf16[2,2,2,128,128]{4,3,2,1,0:T(8,128)(2,1)S(1)}, u32[]{:S(2)}, u32[]{:S(2)}) %collective-permute-start.2) | collective-permute-done | bytes 262176 | tf_op jit(solution)/shard_map/ppermute | solution.py:453
  21.5 0.0 collective-permute-done.3.rest_2_.rest_6_
  21.5 1.3 %collective-permute-start.6 = (bf16[2,2,2,128,128]{4,3,2,1,0:T(8,128)(2,1)S(1)}, bf16[2,2,2,128,128]{4,3,2,1,0:T(8,128)(2,1)S(1)}, u32[]{:S(2)}, u32[]{:S(2)}) collective-permute-start(bf16[2,2,2,128,128]{4,3,2,1,0:T(8,128)(2,1)S(1)} %collective-permute-done.3.rest_2_.rest_6_), channel_id=1, source_target_pairs={{0,8},{8,16},{16,24},{1,9},{9,17},{17,25},{2,10},{10,18},{18,26},{... | collective-permute-start | bytes 786440 | tf_op jit(solution)/shard_map/ppermute | solution.py:459
  22.8 2.5 %collective-permute-start.5 = (bf16[2,2,2,128,128]{4,3,2,1,0:T(8,128)(2,1)S(1)}, bf16[2,2,2,128,128]{4,3,2,1,0:T(8,128)(2,1)}, u32[]{:S(2)}, u32[]{:S(2)}) collective-permute-start(bf16[2,2,2,128,128]{4,3,2,1,0:T(8,128)(2,1)S(1)} %collective-permute-done.3.rest_2_.rest_6_), channel_id=1, source_target_pairs={{0,2},{1,3},{2,0},{3,1},{4,6},{5,7},{6,4},{7,5},{8,10},{9,11},{10,... | collective-permute-start | bytes 786440 | tf_op jit(solution)/shard_map/ppermute | solution.py:453
  25.4 1.4 %copy.15.key_blocks = s32[32,12]{1,0:T(8,128)} copy(s32[32,12]{0,1:T(8,128)} %param.12) | data formatting | bytes 3072 | tf_op args[4]
  26.7 2.2 %collective-permute-done.6.rest_2_ = bf16[2,2,2,128,128]{4,3,2,1,0:T(8,128)(2,1)S(1)} collective-permute-done((bf16[2,2,2,128,128]{4,3,2,1,0:T(8,128)(2,1)S(1)}, bf16[2,2,2,128,128]{4,3,2,1,0:T(8,128)(2,1)S(1)}, u32[]{:S(2)}, u32[]{:S(2)}) %collective-permute-start.6) | collective-permute-done | bytes 262176 | tf_op jit(solution)/shard_map/ppermute | solution.py:459
  29.0 1.3 %collective-permute-start.7 = (bf16[2,2,2,128,128]{4,3,2,1,0:T(8,128)(2,1)S(1)}, bf16[2,2,2,128,128]{4,3,2,1,0:T(8,128)(2,1)S(1)}, u32[]{:S(2)}, u32[]{:S(2)}) collective-permute-start(bf16[2,2,2,128,128]{4,3,2,1,0:T(8,128)(2,1)S(1)} %collective-permute-done.2.rest_1_.rest_5_), channel_id=1, source_target_pairs={{0,8},{8,16},{16,24},{1,9},{9,17},{17,25},{2,10},{10,18},{18,26},{... | collective-permute-start | bytes 786440 | tf_op jit(solution)/shard_map/ppermute | solution.py:459
  30.2 3.8 %collective-permute-start.8 = (bf16[2,2,2,128,128]{4,3,2,1,0:T(8,128)(2,1)S(1)}, bf16[2,2,2,128,128]{4,3,2,1,0:T(8,128)(2,1)S(1)}, u32[]{:S(2)}, u32[]{:S(2)}) collective-permute-start(bf16[2,2,2,128,128]{4,3,2,1,0:T(8,128)(2,1)S(1)} %collective-permute-done.6.rest_2_), channel_id=1, source_target_pairs={{0,2},{1,3},{2,0},{3,1},{4,6},{5,7},{6,4},{7,5},{8,10},{9,11},{10,... | collective-permute-start | bytes 786440 | tf_op jit(solution)/shard_map/ppermute | solution.py:453
  34.0 0.0 collective-permute-done.5.rest_3_.rest_7_
  34.0 0.0 collective-permute-done.1.other
  34.0 0.0 copy-start.2
  34.0 1.2 %copy-done.2 = bf16[2,2,8,128,128]{4,3,2,1,0:T(8,128)(2,1)S(1)} copy-done((bf16[2,2,8,128,128]{4,3,2,1,0:T(8,128)(2,1)S(1)}, bf16[2,2,8,128,128]{4,3,2,1,0:T(8,128)(2,1)}, u32[]{:S(2)}) %copy-start.2) | copy-done | bytes 1048600
  35.2 0.0 copy-start.3
  35.3 3.2 %current_statistics.1 = (bf16[2,2,2,128,1024]{4,3,2,1,0:T(8,128)(2,1)S(1)}, f32[2,2,8,1024]{3,2,1,0:T(8,128)S(1)}) custom-call(s32[32,12]{1,0:T(8,128)} %copy.15.key_blocks, s32[32]{0:T(128)} %key_counts.9, bf16[2,2,8,128,128]{4,3,2,1,0:T(8,128)(2,1)S(1)} %copy-done.2, bf16[2,2,8,128,128]{4,3,2,1,0:T(8,128)(2,1)S(1)} %collective-permute-done.1.other, ...), custom_call_target="tpu_custom_call" | custom-call | flops 6000000000 | bytes 1048576 | tf_op jit(solution)/shard_map/current_statistics/pallas_call | solution.py:90
  38.5 0.0 collective-permute-done.7.rest_1_
  38.5 0.0 collective-permute-done.8.rest_3_
  38.5 0.0 copy-done.3
  38.5 17.9 %previous_gradients.1 = (bf16[2,2,2,128,128]{4,3,2,1,0:T(8,128)(2,1)S(1)}, bf16[2,2,2,128,128]{4,3,2,1,0:T(8,128)(2,1)S(1)}, bf16[2,2,2,128,128]{4,3,2,1,0:T(8,1...) custom-call(s32[32,12]{1,0:T(8,128)} %copy.15.key_blocks, ...), custom_call_target="tpu_custom_call" | custom-call | flops 14000000000 | bytes 1048576 | tf_op jit(solution)/shard_map/previous_gradients/pallas_call | solution.py:90
  56.4 1.3 %collective-permute-start.9 = (bf16[2,2,2,128,128]{4,3,2,1,0:T(8,128)(2,1)S(1)}, bf16[2,2,2,128,128]{4,3,2,1,0:T(8,128)(2,1)S(1)}, u32[]{:S(2)}, u32[]{:S(2)}) collective-permute-start(bf16[2,2,2,128,128]{4,3,2,1,0:T(8,128)(2,1)S(1)} %get-tuple-element.68), channel_id=1, source_target_pairs={{8,0},{16,8},{24,16},{9,1},{17,9},{25,17},{10,2},{18,10},{26,18},{... | collective-permute-start | bytes 786440 | tf_op jit(solution)/shard_map/ppermute | solution.py:462
  57.8 0.1 collective-permute-start.10
  57.8 0.0 copy-start
  57.9 6.0 %current_gradients.1 = (f32[2,2,2,128,128]{4,3,2,1,0:T(8,128)S(1)}, f32[2,2,2,128,128]{4,3,2,1,0:T(8,128)S(1)}, f32[2,2,2,128,128]{4,3,2,1,0:T(8,128)S(1)}, bf16...) custom-call(s32[32,12]{1,0:T(8,128)} %copy.15.key_blocks, s32[32]{0:T(128)} %key_counts.9, ...), custom_call_target="tpu_custom_call" | custom-call | flops 10000000000 | bytes 1048576 | tf_op jit(solution)/shard_map/current_gradients/pallas_call | solution.py:90
  63.8 3.2 %collective-permute-start.12 = (bf16[2,2,2,128,128]{4,3,2,1,0:T(8,128)(2,1)S(1)}, bf16[2,2,2,128,128]{4,3,2,1,0:T(8,128)(2,1)S(1)}, u32[]{:S(2)}, u32[]{:S(2)}) collective-permute-start(bf16[2,2,2,128,128]{4,3,2,1,0:T(8,128)(2,1)S(1)} %get-tuple-element.81), channel_id=1, source_target_pairs={{0,2},{1,3},{2,0},{3,1},{4,6},{5,7},{6,4},{7,5},{8,10},{9,11},{10,... | collective-permute-start | bytes 786440 | tf_op jit(solution)/shard_map/ppermute | solution.py:453
  67.1 0.0 collective-permute-done.9
  67.1 0.1 add_convert_fusion.2
  67.1 0.1 collective-permute-start.16
  67.2 0.0 collective-permute-done.10
  67.2 0.1 add_convert_fusion.1
  67.3 1.3 %collective-permute-start.11 = (bf16[2,2,2,128,128]{4,3,2,1,0:T(8,128)(2,1)S(1)}, bf16[2,2,2,128,128]{4,3,2,1,0:T(8,128)(2,1)S(1)}, u32[]{:S(2)}, u32[]{:S(2)}) collective-permute-start(bf16[2,2,2,128,128]{4,3,2,1,0:T(8,128)(2,1)S(1)} %add_convert_fusion.1), channel_id=1, source_target_pairs={{8,0},{16,8},{24,16},{9,1},{17,9},{25,17},{10,2},{18,10},{26,18},{... | collective-permute-start | bytes 786440 | tf_op jit(solution)/shard_map/ppermute | solution.py:462
  68.6 1.3 %collective-permute-start.15 = (bf16[2,2,2,128,128]{4,3,2,1,0:T(8,128)(2,1)S(1)}, bf16[2,2,2,128,128]{4,3,2,1,0:T(8,128)(2,1)S(1)}, u32[]{:S(2)}, u32[]{:S(2)}) collective-permute-start(bf16[2,2,2,128,128]{4,3,2,1,0:T(8,128)(2,1)S(1)} %get-tuple-element.89), channel_id=1, source_target_pairs={{8,0},{16,8},{24,16},{9,1},{17,9},{25,17},{10,2},{18,10},{26,18},{... | collective-permute-start | bytes 786440 | tf_op jit(solution)/shard_map/ppermute | solution.py:462
  69.9 0.0 copy-done
  69.9 6.4 %query_results.2 = (bf16[2,128,1024]{2,1,0:T(8,128)(2,1)S(1)}, bf16[2,128,1024]{2,1,0:T(8,128)(2,1)S(1)}) custom-call(s32[32,12]{1,0:T(8,128)} %copy.15.key_blocks, s32[32]{0:T(128)} %key_counts.9, s32[32]{0:T(128)} %place_ref.7, bf16[2,8,2,2,128,1024]{5,4,3,2,1,0:T(8,128)(2,1)} %get-tuple-element.70.far_saved, ...), custom_call_target="tpu_custom_call" | custom-call | flops 20000000000 | bytes 1048576 | tf_op jit(solution)/shard_map/query_results/pallas_call | solution.py:90
  76.4 4.8 %collective-permute-start.13 = (bf16[2,128,1024]{2,1,0:T(8,128)(2,1)S(1)}, bf16[2,128,1024]{2,1,0:T(8,128)(2,1)S(1)}, u32[]{:S(2)}, u32[]{:S(2)}) collective-permute-start(bf16[2,128,1024]{2,1,0:T(8,128)(2,1)S(1)} %get-tuple-element.75), channel_id=1, source_target_pairs={{0,1},{1,0},{2,3},{3,2},{4,5},{5,4},{6,7},{7,6},{8,9},{9,8},{10,11... | collective-permute-start | bytes 1572872 | tf_op jit(solution)/shard_map/ppermute | solution.py:453
  81.2 0.0 collective-permute-done.12
  81.2 0.0 collective-permute-done.11
  81.2 0.1 add_convert_fusion
  81.3 4.3 %collective-permute-start.17 = (bf16[2,2,2,128,128]{4,3,2,1,0:T(8,128)(2,1)S(1)}, bf16[2,2,2,128,128]{4,3,2,1,0:T(8,128)(2,1)S(1)}, u32[]{:S(2)}, u32[]{:S(2)}) collective-permute-start(bf16[2,2,2,128,128]{4,3,2,1,0:T(8,128)(2,1)S(1)} %add_convert_fusion), channel_id=1, source_target_pairs={{0,4},{1,5},{2,6},{3,7},{4,0},{5,1},{6,2},{7,3},{8,12},{9,13},{10,... | collective-permute-start | bytes 786440 | tf_op jit(solution)/shard_map/ppermute | solution.py:453
  85.6 6.4 %query_results.3 = (bf16[2,128,1024]{2,1,0:T(8,128)(2,1)S(1)}, bf16[2,128,1024]{2,1,0:T(8,128)(2,1)S(1)}) custom-call(s32[32,12]{1,0:T(8,128)} %copy.15.key_blocks, s32[32]{0:T(128)} %key_counts.9, s32[32]{0:T(128)} %place_ref.7, bf16[2,8,2,2,128,1024]{5,4,3,2,1,0:T(8,128)(2,1)} %get-tuple-element.70.far_saved, ...), custom_call_target="tpu_custom_call" | custom-call | flops 20000000000 | bytes 1048576 | tf_op jit(solution)/shard_map/query_results/pallas_call | solution.py:90
  92.0 0.3 collective-permute-start.14
  92.4 0.0 collective-permute-done.15.rest_1_
  92.4 0.0 collective-permute-done.16.rest_2_
  92.4 5.5 %collective-permute-done.17.rest_3_ = bf16[2,2,2,128,128]{4,3,2,1,0:T(8,128)(2,1)S(1)} collective-permute-done((bf16[2,2,2,128,128]{4,3,2,1,0:T(8,128)(2,1)S(1)}, bf16[2,2,2,128,128]{4,3,2,1,0:T(8,128)(2,1)S(1)}, u32[]{:S(2)}, u32[]{:S(2)}) %collective-permute-start.17) | collective-permute-done | bytes 262176 | tf_op jit(solution)/shard_map/ppermute | solution.py:453
  97.9 0.9 key_gradients.1
  98.7 0.7 collective-permute-start.18
  99.4 1.0 collective-permute-done.18.refs_1_
  100.4 0.7 join_keys.1
  101.1 0.0 collective-permute-done.13.refs_2_
  101.1 0.0 collective-permute-done.14.refs_3_
  101.1 1.5 %join_queries.1 = (bf16[128,4096]{1,0:T(8,128)(2,1)}, bf16[128,4096]{1,0:T(8,128)(2,1)}) custom-call(bf16[2,128,1024]{2,1,0:T(8,128)(2,1)S(1)} %get-tuple-element.72.refs_0_, bf16[2,128,1024]{2,1,0:T(8,128)(2,1)S(1)} %get-tuple-element.84.refs_1_, bf16[2,128,1024]{2,1,0:T(8,128)(2,1)S(1)} %collective-permute-done.13.refs_2_, ...), custom_call_target="tpu_custom_call" | custom-call | flops 2000000000 | bytes 1048576 | tf_op jit(solution)/shard_map/join_queries/pallas_call | solution.py:90
  (1 shorter events, 0.0 us)
Async XLA Ops:
  2.5 4.7 %collective-permute-start = (bf16[2,2,128,128]{3,2,1,0:T(8,128)(2,1)S(1)}, bf16[2,2,128,128]{3,2,1,0:T(8,128)(2,1)S(1)}, u32[]{:S(2)}, u32[]{:S(2)}) collective-permute-start(bf16[2,2,128,128]{3,2,1,0:T(8,128)(2,1)S(1)} %get-tuple-element.53), channel_id=1, source_target_pairs={{0,1},{1,0},{2,3},{3,2},{4,5},{5,4},{6,7},{7,6},{8,9},{9,8},{10,11... | collective-permute-start | bytes 393224 | tf_op jit(solution)/shard_map/ppermute | solution.py:453
  6.3 1.0 copy-start.1
  7.2 26.8 %collective-permute-start.1 = (bf16[2,2,8,128,128]{4,3,2,1,0:T(8,128)(2,1)S(1)}, bf16[2,2,8,128,128]{4,3,2,1,0:T(8,128)(2,1)S(1)}, u32[]{:S(2)}, u32[]{:S(2)}) collective-permute-start(bf16[2,2,8,128,128]{4,3,2,1,0:T(8,128)(2,1)S(1)} %get-tuple-element.56), channel_id=1, source_target_pairs={{0,1},{1,0},{2,3},{3,2},{4,5},{5,4},{6,7},{7,6},{8,9},{9,8},{10,11... | collective-permute-start | bytes 3145736 | tf_op jit(solution)/shard_map/ppermute | solution.py:453
  7.3 9.3 %collective-permute-start.4 = (bf16[2,2,2,128,128]{4,3,2,1,0:T(8,128)(2,1)S(1)}, bf16[2,2,2,128,128]{4,3,2,1,0:T(8,128)(2,1)S(1)}, u32[]{:S(2)}, u32[]{:S(2)}) collective-permute-start(bf16[2,2,2,128,128]{4,3,2,1,0:T(8,128)(2,1)S(1)} %pad_maximum_fusion.rest_0_.rest_4_), channel_id=1, source_target_pairs={{0,8},{8,16},{16,24},{1,9},{9,17},{17,25},{2,10},{10,18},{18,26},{... | collective-permute-start | bytes 786440 | tf_op jit(solution)/shard_map/ppermute | solution.py:459
  8.6 13.0 %collective-permute-start.2 = (bf16[2,2,2,128,128]{4,3,2,1,0:T(8,128)(2,1)S(1)}, bf16[2,2,2,128,128]{4,3,2,1,0:T(8,128)(2,1)S(1)}, u32[]{:S(2)}, u32[]{:S(2)}) collective-permute-start(bf16[2,2,2,128,128]{4,3,2,1,0:T(8,128)(2,1)S(1)} %pad_maximum_fusion.rest_0_.rest_4_), channel_id=1, source_target_pairs={{0,2},{1,3},{2,0},{3,1},{4,6},{5,7},{6,4},{7,5},{8,10},{9,11},{10,... | collective-permute-start | bytes 786440 | tf_op jit(solution)/shard_map/ppermute | solution.py:453
  9.9 11.6 %collective-permute-start.3 = (bf16[2,2,2,128,128]{4,3,2,1,0:T(8,128)(2,1)S(1)}, bf16[2,2,2,128,128]{4,3,2,1,0:T(8,128)(2,1)S(1)}, u32[]{:S(2)}, u32[]{:S(2)}) collective-permute-start(bf16[2,2,2,128,128]{4,3,2,1,0:T(8,128)(2,1)S(1)} %pad_maximum_fusion.rest_0_.rest_4_), channel_id=1, source_target_pairs={{0,4},{1,5},{2,6},{3,7},{4,0},{5,1},{6,2},{7,3},{8,12},{9,13},{10,... | collective-permute-start | bytes 786440 | tf_op jit(solution)/shard_map/ppermute | solution.py:453
  21.5 7.4 %collective-permute-start.6 = (bf16[2,2,2,128,128]{4,3,2,1,0:T(8,128)(2,1)S(1)}, bf16[2,2,2,128,128]{4,3,2,1,0:T(8,128)(2,1)S(1)}, u32[]{:S(2)}, u32[]{:S(2)}) collective-permute-start(bf16[2,2,2,128,128]{4,3,2,1,0:T(8,128)(2,1)S(1)} %collective-permute-done.3.rest_2_.rest_6_), channel_id=1, source_target_pairs={{0,8},{8,16},{16,24},{1,9},{9,17},{17,25},{2,10},{10,18},{18,26},{... | collective-permute-start | bytes 786440 | tf_op jit(solution)/shard_map/ppermute | solution.py:459
  22.8 11.2 %collective-permute-start.5 = (bf16[2,2,2,128,128]{4,3,2,1,0:T(8,128)(2,1)S(1)}, bf16[2,2,2,128,128]{4,3,2,1,0:T(8,128)(2,1)}, u32[]{:S(2)}, u32[]{:S(2)}) collective-permute-start(bf16[2,2,2,128,128]{4,3,2,1,0:T(8,128)(2,1)S(1)} %collective-permute-done.3.rest_2_.rest_6_), channel_id=1, source_target_pairs={{0,2},{1,3},{2,0},{3,1},{4,6},{5,7},{6,4},{7,5},{8,10},{9,11},{10,... | collective-permute-start | bytes 786440 | tf_op jit(solution)/shard_map/ppermute | solution.py:453
  29.0 9.5 %collective-permute-start.7 = (bf16[2,2,2,128,128]{4,3,2,1,0:T(8,128)(2,1)S(1)}, bf16[2,2,2,128,128]{4,3,2,1,0:T(8,128)(2,1)S(1)}, u32[]{:S(2)}, u32[]{:S(2)}) collective-permute-start(bf16[2,2,2,128,128]{4,3,2,1,0:T(8,128)(2,1)S(1)} %collective-permute-done.2.rest_1_.rest_5_), channel_id=1, source_target_pairs={{0,8},{8,16},{16,24},{1,9},{9,17},{17,25},{2,10},{10,18},{18,26},{... | collective-permute-start | bytes 786440 | tf_op jit(solution)/shard_map/ppermute | solution.py:459
  30.2 8.3 %collective-permute-start.8 = (bf16[2,2,2,128,128]{4,3,2,1,0:T(8,128)(2,1)S(1)}, bf16[2,2,2,128,128]{4,3,2,1,0:T(8,128)(2,1)S(1)}, u32[]{:S(2)}, u32[]{:S(2)}) collective-permute-start(bf16[2,2,2,128,128]{4,3,2,1,0:T(8,128)(2,1)S(1)} %collective-permute-done.6.rest_2_), channel_id=1, source_target_pairs={{0,2},{1,3},{2,0},{3,1},{4,6},{5,7},{6,4},{7,5},{8,10},{9,11},{10,... | collective-permute-start | bytes 786440 | tf_op jit(solution)/shard_map/ppermute | solution.py:453
  34.0 1.2 %copy-start.2 = (bf16[2,2,8,128,128]{4,3,2,1,0:T(8,128)(2,1)S(1)}, bf16[2,2,8,128,128]{4,3,2,1,0:T(8,128)(2,1)}, u32[]{:S(2)}) copy-start(bf16[2,2,8,128,128]{4,3,2,1,0:T(8,128)(2,1)} %copy-done.1) | copy-start | bytes 3145732
  35.2 3.3 %copy-start.3 = (bf16[2,2,8,128,128]{4,3,2,1,0:T(8,128)(2,1)S(1)}, bf16[2,2,8,128,128]{4,3,2,1,0:T(8,128)(2,1)}, u32[]{:S(2)}) copy-start(bf16[2,2,8,128,128]{4,3,2,1,0:T(8,128)(2,1)} %copy-done.1) | copy-start | bytes 3145732
  56.4 10.6 %collective-permute-start.9 = (bf16[2,2,2,128,128]{4,3,2,1,0:T(8,128)(2,1)S(1)}, bf16[2,2,2,128,128]{4,3,2,1,0:T(8,128)(2,1)S(1)}, u32[]{:S(2)}, u32[]{:S(2)}) collective-permute-start(bf16[2,2,2,128,128]{4,3,2,1,0:T(8,128)(2,1)S(1)} %get-tuple-element.68), channel_id=1, source_target_pairs={{8,0},{16,8},{24,16},{9,1},{17,9},{25,17},{10,2},{18,10},{26,18},{... | collective-permute-start | bytes 786440 | tf_op jit(solution)/shard_map/ppermute | solution.py:462
  57.8 9.5 %collective-permute-start.10 = (bf16[2,2,2,128,128]{4,3,2,1,0:T(8,128)(2,1)S(1)}, bf16[2,2,2,128,128]{4,3,2,1,0:T(8,128)(2,1)S(1)}, u32[]{:S(2)}, u32[]{:S(2)}) collective-permute-start(bf16[2,2,2,128,128]{4,3,2,1,0:T(8,128)(2,1)S(1)} %get-tuple-element.79), channel_id=1, source_target_pairs={{0,2},{1,3},{2,0},{3,1},{4,6},{5,7},{6,4},{7,5},{8,10},{9,11},{10,... | collective-permute-start | bytes 786440 | tf_op jit(solution)/shard_map/ppermute | solution.py:453
  57.8 12.1 %copy-start = (f32[320,128]{1,0:T(8,128)S(1)}, f32[320,128]{1,0:T(8,128)}, u32[]{:S(2)}) copy-start(f32[320,128]{1,0:T(8,128)} %constant.2.clone.refs_2_.rest_8_.rest_4_) | copy-start | bytes 491524
  63.8 17.4 %collective-permute-start.12 = (bf16[2,2,2,128,128]{4,3,2,1,0:T(8,128)(2,1)S(1)}, bf16[2,2,2,128,128]{4,3,2,1,0:T(8,128)(2,1)S(1)}, u32[]{:S(2)}, u32[]{:S(2)}) collective-permute-start(bf16[2,2,2,128,128]{4,3,2,1,0:T(8,128)(2,1)S(1)} %get-tuple-element.81), channel_id=1, source_target_pairs={{0,2},{1,3},{2,0},{3,1},{4,6},{5,7},{6,4},{7,5},{8,10},{9,11},{10,... | collective-permute-start | bytes 786440 | tf_op jit(solution)/shard_map/ppermute | solution.py:453
  67.1 25.2 %collective-permute-start.16 = (bf16[2,2,2,128,128]{4,3,2,1,0:T(8,128)(2,1)S(1)}, bf16[2,2,2,128,128]{4,3,2,1,0:T(8,128)(2,1)S(1)}, u32[]{:S(2)}, u32[]{:S(2)}) collective-permute-start(bf16[2,2,2,128,128]{4,3,2,1,0:T(8,128)(2,1)S(1)} %add_convert_fusion.2), channel_id=1, source_target_pairs={{0,2},{1,3},{2,0},{3,1},{4,6},{5,7},{6,4},{7,5},{8,10},{9,11},{10,... | collective-permute-start | bytes 786440 | tf_op jit(solution)/shard_map/ppermute | solution.py:453
  67.3 13.9 %collective-permute-start.11 = (bf16[2,2,2,128,128]{4,3,2,1,0:T(8,128)(2,1)S(1)}, bf16[2,2,2,128,128]{4,3,2,1,0:T(8,128)(2,1)S(1)}, u32[]{:S(2)}, u32[]{:S(2)}) collective-permute-start(bf16[2,2,2,128,128]{4,3,2,1,0:T(8,128)(2,1)S(1)} %add_convert_fusion.1), channel_id=1, source_target_pairs={{8,0},{16,8},{24,16},{9,1},{17,9},{25,17},{10,2},{18,10},{26,18},{... | collective-permute-start | bytes 786440 | tf_op jit(solution)/shard_map/ppermute | solution.py:462
  68.6 23.8 %collective-permute-start.15 = (bf16[2,2,2,128,128]{4,3,2,1,0:T(8,128)(2,1)S(1)}, bf16[2,2,2,128,128]{4,3,2,1,0:T(8,128)(2,1)S(1)}, u32[]{:S(2)}, u32[]{:S(2)}) collective-permute-start(bf16[2,2,2,128,128]{4,3,2,1,0:T(8,128)(2,1)S(1)} %get-tuple-element.89), channel_id=1, source_target_pairs={{8,0},{16,8},{24,16},{9,1},{17,9},{25,17},{10,2},{18,10},{26,18},{... | collective-permute-start | bytes 786440 | tf_op jit(solution)/shard_map/ppermute | solution.py:462
  76.4 24.7 %collective-permute-start.13 = (bf16[2,128,1024]{2,1,0:T(8,128)(2,1)S(1)}, bf16[2,128,1024]{2,1,0:T(8,128)(2,1)S(1)}, u32[]{:S(2)}, u32[]{:S(2)}) collective-permute-start(bf16[2,128,1024]{2,1,0:T(8,128)(2,1)S(1)} %get-tuple-element.75), channel_id=1, source_target_pairs={{0,1},{1,0},{2,3},{3,2},{4,5},{5,4},{6,7},{7,6},{8,9},{9,8},{10,11... | collective-permute-start | bytes 1572872 | tf_op jit(solution)/shard_map/ppermute | solution.py:453
  81.3 16.5 %collective-permute-start.17 = (bf16[2,2,2,128,128]{4,3,2,1,0:T(8,128)(2,1)S(1)}, bf16[2,2,2,128,128]{4,3,2,1,0:T(8,128)(2,1)S(1)}, u32[]{:S(2)}, u32[]{:S(2)}) collective-permute-start(bf16[2,2,2,128,128]{4,3,2,1,0:T(8,128)(2,1)S(1)} %add_convert_fusion), channel_id=1, source_target_pairs={{0,4},{1,5},{2,6},{3,7},{4,0},{5,1},{6,2},{7,3},{8,12},{9,13},{10,... | collective-permute-start | bytes 786440 | tf_op jit(solution)/shard_map/ppermute | solution.py:453
  92.0 9.1 %collective-permute-start.14 = (bf16[2,128,1024]{2,1,0:T(8,128)(2,1)S(1)}, bf16[2,128,1024]{2,1,0:T(8,128)(2,1)S(1)}, u32[]{:S(2)}, u32[]{:S(2)}) collective-permute-start(bf16[2,128,1024]{2,1,0:T(8,128)(2,1)S(1)} %get-tuple-element.85), channel_id=1, source_target_pairs={{0,1},{1,0},{2,3},{3,2},{4,5},{5,4},{6,7},{7,6},{8,9},{9,8},{10,11... | collective-permute-start | bytes 1572872 | tf_op jit(solution)/shard_map/ppermute | solution.py:453
  98.7 1.7 %collective-permute-start.18 = (bf16[2,128,256]{2,1,0:T(8,128)(2,1)S(1)}, bf16[2,128,256]{2,1,0:T(8,128)(2,1)S(1)}, u32[]{:S(2)}, u32[]{:S(2)}) collective-permute-start(bf16[2,128,256]{2,1,0:T(8,128)(2,1)S(1)} %get-tuple-element.91), channel_id=1, source_target_pairs={{0,1},{1,0},{2,3},{3,2},{4,5},{5,4},{6,7},{7,6},{8,9},{9,8},{10,11... | collective-permute-start | bytes 393224 | tf_op jit(solution)/shard_map/ppermute | solution.py:453
